TPU v7x, 256 devices: a whole 4x4x8 slice. The times are simulated.
256 devices in a mesh: limb: 8 (over y, z_hi), coef: 32 (over z_lo, x, core).
Axes of the slice: x: 4, y: 4, z: 8 (z_hi: 2, z_lo: 4; z = z_hi * 4 + z_lo), core: 2. Of those that a mesh axis runs over, the one named last changes fastest.
Arguments:
- first_cipher: float32 [16, 2, 2, 32768], P('limb', None, None, 'coef'), may hold values from -0.375 to 0.375
- second_cipher: float32 [16, 2, 2, 32768], P('limb', None, None, 'coef'), may hold values from -0.375 to 0.375
- to_special: float32 [16, 16], replicated, may hold values from -1.5 to 1.5
- keep_table: float32 [16, 16], P(None, 'limb'), may hold values from -1 to 1
- scale_table: float32 [16, 16], P(None, 'limb'), may hold values from -1 to 1
Outputs:
- product: float32 [16, 2, 3, 32768], P('limb', None, None, 'coef')
All inputs are finite; a program needn't handle non-finite values.
Results may differ from a plain program's by a relative error of at most 0.00012.
Values sent between devices are 32-bit elements; how exact they have to be, the bound alone decides.
No kernel may reach another device: no remote copies, remote signals or barrier semaphores. Data moves between devices by JAX's collectives and lax.ppermute only.
A program may use at most 64 MiB of HBM per device.

v0:
```python
import jax
import jax.numpy as jnp
from jax import lax
from jax.sharding import PartitionSpec as P

N2 = 256


highest = lax.Precision.HIGHEST
full_turn = 6.283185307179586


def phase_table(first_index, second_index, modulus):
    product = first_index[:, None] * second_index[None, :] % modulus
    return product.astype(jnp.float32) * (full_turn / modulus)


def twist_apply(real_part, imag_part, angle_table, direction_sign):
    cosine = jnp.cos(angle_table)
    sine_part = jnp.sin(angle_table) * direction_sign
    return (cosine * real_part + sine_part * imag_part, cosine * imag_part - sine_part * real_part)


def spin_rows(real_part, imag_part, angle_table, direction_sign):
    cosine = jnp.cos(angle_table)
    sine_part = jnp.sin(angle_table) * direction_sign

    def row_product(matrix, operand):
        return jnp.einsum("kn,lpbnm->lpbkm", matrix, operand, precision=highest)

    new_real = row_product(cosine, real_part) + row_product(sine_part, imag_part)
    new_imag = row_product(cosine, imag_part) - row_product(sine_part, real_part)
    return (new_real, new_imag)


def spin_columns(real_part, imag_part, angle_table, direction_sign):
    cosine = jnp.cos(angle_table)
    sine_part = jnp.sin(angle_table) * direction_sign

    def column_product(matrix, operand):
        return jnp.einsum("lpbrm,km->lpbrk", operand, matrix, precision=highest)

    new_real = column_product(cosine, real_part) + column_product(sine_part, imag_part)
    new_imag = column_product(cosine, imag_part) - column_product(sine_part, real_part)
    return (new_real, new_imag)


def twist_position(row_total, column_index):
    row_index = jnp.arange(row_total, dtype=jnp.int32)
    length = row_total * N2
    position = row_index[:, None] * N2 + column_index[None, :]
    return position.astype(jnp.float32) * (full_turn / (2 * length))


def forward_spectrum(values, column_start):
    row_total = values.shape[3]
    column_width = values.shape[4]
    length = row_total * N2
    row_index = jnp.arange(row_total, dtype=jnp.int32)
    column_index = column_start + jnp.arange(column_width, dtype=jnp.int32)
    position = twist_position(row_total, column_index)
    real_part = values * jnp.cos(position)
    imag_part = values * jnp.sin(position)
    real_part, imag_part = spin_rows(
        real_part, imag_part, phase_table(row_index, row_index, row_total), 1.0
    )
    real_part, imag_part = twist_apply(
        real_part, imag_part, phase_table(row_index, column_index, length), 1.0
    )
    stacked = jnp.stack([real_part, imag_part])
    exchanged = lax.all_to_all(stacked, "coef", split_axis=4, concat_axis=5, tiled=True)
    real_part, imag_part = (exchanged[0], exchanged[1])
    full_index = jnp.arange(N2, dtype=jnp.int32)
    return spin_columns(real_part, imag_part, phase_table(full_index, full_index, N2), 1.0)


def inverse_spectrum(real_part, imag_part, column_start):
    full_index = jnp.arange(N2, dtype=jnp.int32)
    real_part, imag_part = spin_columns(
        real_part, imag_part, phase_table(full_index, full_index, N2), -1.0
    )
    stacked = jnp.stack([real_part, imag_part])
    exchanged = lax.all_to_all(stacked, "coef", split_axis=5, concat_axis=4, tiled=True)
    real_part, imag_part = (exchanged[0], exchanged[1])
    row_total = real_part.shape[3]
    column_width = real_part.shape[4]
    length = row_total * N2
    row_index = jnp.arange(row_total, dtype=jnp.int32)
    column_index = column_start + jnp.arange(column_width, dtype=jnp.int32)
    real_part, imag_part = twist_apply(
        real_part, imag_part, phase_table(row_index, column_index, length), -1.0
    )
    real_part, imag_part = spin_rows(
        real_part, imag_part, phase_table(row_index, row_index, row_total), -1.0
    )
    position = twist_position(row_total, column_index)
    return (jnp.cos(position) * real_part + jnp.sin(position) * imag_part) / length


def complex_product(left_pair, right_pair):
    return (
        left_pair[0] * right_pair[0] - left_pair[1] * right_pair[1],
        left_pair[0] * right_pair[1] + left_pair[1] * right_pair[0],
    )


def tensor_spectra(spec_real, spec_imag):
    first_low = (spec_real[:, :, 0], spec_imag[:, :, 0])
    first_high = (spec_real[:, :, 1], spec_imag[:, :, 1])
    second_low = (spec_real[:, :, 2], spec_imag[:, :, 2])
    second_high = (spec_real[:, :, 3], spec_imag[:, :, 3])
    product_low = complex_product(first_low, second_low)
    cross_one = complex_product(first_low, second_high)
    cross_two = complex_product(first_high, second_low)
    product_high = complex_product(first_high, second_high)
    tensor_real = jnp.stack([product_low[0], cross_one[0] + cross_two[0], product_high[0]], axis=2)
    tensor_imag = jnp.stack([product_low[1], cross_one[1] + cross_two[1], product_high[1]], axis=2)
    return (tensor_real, tensor_imag)


def per_device(first_cipher, second_cipher, to_special, keep_table, scale_table):
    limb_count = first_cipher.shape[0]
    pair_count = first_cipher.shape[1]
    local_length = first_cipher.shape[3]
    special_count = scale_table.shape[1]
    row_block = local_length // N2
    limb_rank = lax.axis_index("limb")
    coef_rank = lax.axis_index("coef")
    column_width = N2 // lax.axis_size("coef")
    polynomials = jnp.concatenate([first_cipher, second_cipher], axis=2)
    polynomials = polynomials.reshape(limb_count, pair_count, 4, row_block, N2)
    own_rows = lax.dynamic_slice_in_dim(to_special, limb_rank * special_count, special_count, 0)
    joined = jnp.concatenate(
        [
            polynomials,
            jnp.einsum(
                "pq,qabrw->pabrw",
                own_rows,
                lax.all_gather(polynomials, "limb", axis=0, tiled=True),
                precision=highest,
            ),
        ],
        axis=0,
    )
    spread = lax.all_to_all(joined, "coef", split_axis=4, concat_axis=3, tiled=True)
    spec_real, spec_imag = forward_spectrum(spread, coef_rank * column_width)
    tensor_real, tensor_imag = tensor_spectra(spec_real, spec_imag)
    tensor = inverse_spectrum(tensor_real, tensor_imag, coef_rank * column_width)
    natural = lax.all_to_all(tensor, "coef", split_axis=3, concat_axis=4, tiled=True)
    kept = jnp.einsum("iq,qabrw->iabrw", keep_table, natural[:limb_count], precision=highest)
    scaled = jnp.einsum("ip,pabrw->iabrw", scale_table, natural[limb_count:], precision=highest)
    result = lax.psum_scatter(kept + scaled, "limb", scatter_dimension=0, tiled=True)
    return result.reshape(limb_count, pair_count, 3, local_length)


def solution(mesh):
    return jax.shard_map(
        per_device,
        mesh=mesh,
        in_specs=(
            P("limb", None, None, "coef"),
            P("limb", None, None, "coef"),
            P(),
            P(None, "limb"),
            P(None, "limb"),
        ),
        out_specs=P("limb", None, None, "coef"),
        check_vma=False,
    )
```

profile of v0, /device:TPU:2, one launch (start us, length us, event | category | flops | bytes accessed | tf_op | source)
XLA Modules:
  0.0 376.4 jit_solution(1341040472307867954)
XLA Ops:
  7.4 51.2 %all_gather.3 = f32[16,2,4,4,256]{4,3,2,1,0:T(4,128)S(1)} all-gather(f32[2,2,4,4,256]{4,3,2,1,0:T(4,128)S(1)} %reshape.154), channel_id=1, replica_groups=mesh['limb'=8,'coef'=32] {'limb'}, dimensions={0}, use_global_device_ids=true | all-gather | bytes 589824 | tf_op jit(solution)/shard_map/all_gather | solution.py:139
  59.4 3.4 copy.76
  62.9 7.0 %reshape.168 = f32[32,1,1024]{2,1,0:T(1,128)} reshape(f32[256,2,4,4,4]{4,3,2,1,0:T(4,128)} %bitcast.152) | data formatting | bytes 262144
  69.9 8.3 %all-to-all-start = ((f32[32,1,1024]{2,1,0:T(1,128)}), f32[32,1,1024]{2,1,0:T(1,128)S(1)}, u32[]{:S(2)}, u32[]{:S(2)}) async-start(f32[32,1,1024]{2,1,0:T(1,128)} %reshape.168), calls=%async_computation | async-start | bytes 262144 | tf_op jit(solution)/shard_map/all_to_all | solution.py:145
  78.6 7.1 %all-to-all-done = f32[32,1,1024]{2,1,0:T(1,128)S(1)} async-done(((f32[32,1,1024]{2,1,0:T(1,128)}), f32[32,1,1024]{2,1,0:T(1,128)S(1)}, u32[]{:S(2)}, u32[]{:S(2)}) %all-to-all-start) | async-done | bytes 131104 | tf_op jit(solution)/shard_map/all_to_all | solution.py:145
  87.2 6.8 %reshape.169 = f32[256,2,4,4,4]{4,3,2,1,0:T(4,128)} reshape(f32[32,1024]{1,0:T(8,128)S(1)} %reduce) | data formatting | bytes 262144
  94.0 9.1 %copy.123 = f32[4,2,4,4,32,8]{5,4,3,2,1,0:T(8,128)S(1)} copy(f32[4,2,4,4,32,8]{0,3,2,1,5,4:T(4,128)} %bitcast.153) | data formatting | bytes 262144 | tf_op jit(solution)/shard_map/all_to_all | solution.py:145
  103.1 1.8 copy.78
  104.9 3.4 fusion.2
  108.3 3.4 fusion
  111.7 3.4 fusion.12
  115.1 3.4 add_bitcast_fusion
  118.5 3.3 copy.85
  121.8 6.7 %reshape.170 = f32[32,1,2048]{2,1,0:T(1,128)S(1)} reshape(f32[128,2,4,2,4,8]{5,4,3,2,1,0:T(4,128)} %bitcast.154) | data formatting | bytes 524288
  128.6 14.2 %all_to_all.63 = f32[32,1,2048]{2,1,0:T(1,128)S(1)} all-to-all(f32[32,1,2048]{2,1,0:T(1,128)S(1)} %reshape.170), channel_id=1, replica_groups=mesh['limb'=8,'coef'=32] {'coef'}, dimensions={0} | all-to-all | bytes 524288 | tf_op jit(solution)/shard_map/all_to_all | solution.py:71
  142.7 1.3 reduce.1
  144.0 6.3 %reshape.171 = f32[128,2,4,2,4,8]{5,4,3,2,1,0:T(4,128)} reshape(f32[32,2048]{1,0:T(8,128)S(1)} %reduce.1) | data formatting | bytes 524288
  150.3 4.6 %copy.86 = f32[2,4,2,4,128,8]{5,4,3,2,1,0:T(8,128)S(1)} copy(f32[2,4,2,4,128,8]{5,3,2,1,0,4:T(4,128)} %bitcast.155) | data formatting | bytes 524288 | tf_op jit(solution)/shard_map/all_to_all | solution.py:71
  154.9 1.8 fusion.185
  157.0 1.1 squeeze.8
  158.1 1.4 fusion.50
  159.5 1.8 copy.88
  161.4 1.1 squeeze.9
  162.5 1.4 fusion.48
  163.9 1.4 convolution_add_fusion.1
  165.3 1.4 convolution_subtract_fusion
  166.8 1.5 fusion.46
  168.3 1.4 fusion.44
  169.7 1.4 fusion.28
  171.1 1.4 fusion.27
  172.5 4.9 %copy.89 = f32[2,4,2,3,4,256]{4,1,3,2,0,5:T(4,128)} copy(f32[2,4,2,3,4,256]{5,4,3,2,1,0:T(4,128)S(1)} %pad_maximum_fusion.1) | data formatting | bytes 393216 | tf_op jit(solution)/shard_map/stack | solution.py:82
  177.5 8.6 %reshape.172 = f32[32,1,1536]{2,1,0:T(1,128)} reshape(f32[256,2,2,3,4,4]{5,4,3,2,1,0:T(4,128)} %bitcast.149) | data formatting | bytes 393216
  186.1 5.4 %all-to-all-start.2 = ((f32[32,1,1536]{2,1,0:T(1,128)}), f32[32,1,1536]{2,1,0:T(1,128)S(1)}, u32[]{:S(2)}, u32[]{:S(2)}) async-start(f32[32,1,1536]{2,1,0:T(1,128)} %reshape.172), calls=%async_computation.2 | async-start | bytes 393216 | tf_op jit(solution)/shard_map/all_to_all | solution.py:83
  191.8 8.3 %all-to-all-done.2 = f32[32,1,1536]{2,1,0:T(1,128)S(1)} async-done(((f32[32,1,1536]{2,1,0:T(1,128)}), f32[32,1,1536]{2,1,0:T(1,128)S(1)}, u32[]{:S(2)}, u32[]{:S(2)}) %all-to-all-start.2) | async-done | bytes 196640 | tf_op jit(solution)/shard_map/all_to_all | solution.py:83
  200.0 1.1 reduce.2
  201.1 9.8 %reshape.173 = f32[256,2,2,3,4,4]{5,4,3,2,1,0:T(4,128)} reshape(f32[32,1536]{1,0:T(8,128)S(1)} %reduce.2) | data formatting | bytes 393216
  211.0 12.7 %copy.124 = f32[2,4,2,3,4,32,8]{6,5,4,3,2,1,0:T(8,128)S(1)} copy(f32[2,4,2,3,4,32,8]{4,1,3,2,0,6,5:T(4,128)} %bitcast.150) | data formatting | bytes 393216 | tf_op jit(solution)/shard_map/all_to_all | solution.py:83
  224.0 1.2 copy.91
  225.2 1.2 copy.93
  226.5 2.6 fusion.36
  229.1 2.6 fusion.35
  231.7 2.6 fusion.26
  234.3 2.6 fusion.24
  237.7 1.8 reshape.174
  239.5 11.8 %all_to_all.64 = f32[32,1,768]{2,1,0:T(1,128)S(1)} all-to-all(f32[32,1,768]{2,1,0:T(1,128)S(1)} %reshape.174), channel_id=1, replica_groups=mesh['limb'=8,'coef'=32] {'coef'}, dimensions={0} | all-to-all | bytes 196608 | tf_op jit(solution)/shard_map/all_to_all | solution.py:149
  252.3 1.9 reshape.175
  256.7 1.0 copy.104
  259.0 108.6 %all-reduce.3.cloned.1.call-done = f32[16,2,3,4,256]{4,3,2,1,0:T(4,128)} async-done(((f32[16,2,3,4,256]{4,3,2,1,0:T(4,128)}), f32[16,2,3,4,256]{4,3,2,1,0:T(4,128)}) %all-reduce.3.cloned.1.call-update) | async-done | bytes 393232
  (46 shorter events, 10.6 us)
Async XLA Ops:
  6.5 52.2 %copy-start = (f32[16,16]{1,0:T(8,128)S(1)}, f32[16,16]{1,0:T(8,128)}, u32[]{:S(2)}) copy-start(f32[16,16]{1,0:T(8,128)} %param.7) | copy-start | bytes 3076
  69.9 15.8 %all-to-all-start = ((f32[32,1,1024]{2,1,0:T(1,128)}), f32[32,1,1024]{2,1,0:T(1,128)S(1)}, u32[]{:S(2)}, u32[]{:S(2)}) async-start(f32[32,1,1024]{2,1,0:T(1,128)} %reshape.168), calls=%async_computation | async-start | bytes 262144 | tf_op jit(solution)/shard_map/all_to_all | solution.py:145
  186.1 14.0 %all-to-all-start.2 = ((f32[32,1,1536]{2,1,0:T(1,128)}), f32[32,1,1536]{2,1,0:T(1,128)S(1)}, u32[]{:S(2)}, u32[]{:S(2)}) async-start(f32[32,1,1536]{2,1,0:T(1,128)} %reshape.172), calls=%async_computation.2 | async-start | bytes 393216 | tf_op jit(solution)/shard_map/all_to_all | solution.py:83
  191.5 176.2 %all-reduce.3.cloned.1.call-start = ((), (), s32[]{:S(2)}) async-start(), calls=%async_computation.4 | async-start | bytes 786432
  254.7 1.0 copy-start.2
  255.1 1.1 copy-start.3
  255.2 2.5 copy-start.4
  255.2 113.9 %copy-start.1 = (f32[16,16]{1,0:T(8,128)S(1)}, f32[16,16]{1,0:T(8,128)}, u32[]{:S(2)}) copy-start(f32[16,16]{1,0:T(8,128)} %param.7) | copy-start | bytes 3076
Sparse Core Ops, SparseCore 0:
  257.9 109.7 all-reduce.2
where the time goes:
time: 382 us; the launch traced here: 376 us
  waiting for transfers between devices  124 us (32%)
  local copies, waits for them, and re-layouts  104 us (27%)
  blocking collectives  77.2 us (20%)
  matrix products  37.1 us (10%)
  between operations  14.9 us (4%)
  starting transfers between devices  13.8 us (4%)
  other arithmetic  5.39 us (1%)
    unnamed x2, waiting for transfers between devices  109 us
    all_gather x1, blocking collectives, per_device(): lax.all_gather(polynomials, 'limb', axis=0, tiled=True)  51.2 us
    unnamed x20, local copies, waits for them, and re-layouts  50.3 us
    dot_general x8, matrix products, row_product(): return jnp.einsum('kn,lpbnm->lpbkm', matrix, operand, precision=highest)  24.1 us
    all_to_all x1, blocking collectives, forward_spectrum(): lax.all_to_all(stacked, 'coef', split_axis=4, concat_axis=5, tiled=True)  14.2 us
    all_to_all x1, local copies, waits for them, and re-layouts, inverse_spectrum(): lax.all_to_all(stacked, 'coef', split_axis=5, concat_axis=4, tiled=True)  12.7 us
    all_to_all x1, blocking collectives, per_device(): lax.all_to_all(tensor, 'coef', split_axis=3, concat_axis=4, tiled=True)  11.8 us
    all_to_all x3, local copies, waits for them, and re-layouts, per_device(): lax.all_to_all(joined, 'coef', split_axis=4, concat_axis=3, tiled=True)  11.4 us
  transfers between devices with their start and end apart: 3, of which 3 were waited for; matrix products, arithmetic and copies ran while one was open for 0% of the time, Pallas kernels for 0%

commit v1 on v0

v1 whole, which is shorter than its diff:
```python
import math

import jax
import jax.numpy as jnp
import ml_dtypes
import numpy as np
from jax import lax
from jax.experimental import pallas as pl
from jax.experimental.pallas import tpu as pltpu
from jax.sharding import PartitionSpec as P

LANES = 128
U = 8
K0 = 8
BLOCK = U * LANES
COEF = 32
GROUPS = 8
ROOTS = 2 * LANES
f32 = jnp.float32
bf16 = jnp.bfloat16


def split_constant(values):
    high = values.astype(np.float32).astype(ml_dtypes.bfloat16)
    low = (values - high.astype(np.float64)).astype(ml_dtypes.bfloat16)
    return high, low


def turn_tables():
    index = np.arange(LANES)
    angle = 2 * np.pi * (index[:, None] * index[None, :] % LANES) / LANES
    wide = np.concatenate([np.cos(angle), np.sin(angle)], axis=1)
    v = np.arange(LANES)[None, :]
    k0 = np.arange(K0)[:, None]
    phase = np.pi * v * (4 * k0 + 1) / 2048
    twiddle = np.concatenate([np.cos(phase), np.sin(phase)], axis=0)
    return split_constant(wide), twiddle.astype(np.float32)


def split_value(values):
    high = values.astype(bf16)
    low = (values - high.astype(f32)).astype(bf16)
    return high, low


def dot3(left, right, dims):
    def one(a, b):
        return lax.dot_general(a, b, (dims, ((), ())), preferred_element_type=f32)

    return one(left[0], right[0]) + (one(left[0], right[1]) + one(left[1], right[0]))


def turn(u, k0):
    angle = math.pi * u * (4 * k0 + 1) / 16
    return math.cos(angle), math.sin(angle)


def evaluate_kernel(first, second, keep, scale, wide_high, wide_low, twiddle, out, held):
    for pair in range(2):
        for u in range(U):
            base = (pair * U + u) * 8
            for limb in range(2):
                for cipher, ref in enumerate((first, second)):
                    held[pl.ds(base + limb * 4 + cipher, 2, stride=2), :] = ref[
                        limb, pair, :, u * LANES : (u + 1) * LANES
                    ]
    rows_real = []
    for pair in range(2):
        parts = [held[(pair * U + u) * 8 : (pair * U + u + 1) * 8, :] for u in range(U)]
        spun = [None] * K0
        for k0 in range(K0 // 2):
            sums = []
            for start in (0, 1):
                real = imag = None
                for u in range(start, U, 2):
                    cosine, sine = turn(u, k0)
                    term_real = parts[u] if u == 0 else parts[u] * cosine
                    real = term_real if real is None else real + term_real
                    if u:
                        term_imag = parts[u] * sine
                        imag = term_imag if imag is None else imag + term_imag
                sums.append((real, imag))
            (even_real, even_imag), (odd_real, odd_imag) = sums
            spun[k0] = (even_real + odd_real, even_imag + odd_imag)
            spun[k0 + K0 // 2] = (even_real - odd_real, even_imag - odd_imag)
        reals, imags = [], []
        for k0 in range(K0):
            cosine = twiddle[k0 : k0 + 1, :]
            sine = twiddle[K0 + k0 : K0 + k0 + 1, :]
            real, imag = spun[k0]
            reals.append(real * cosine - imag * sine)
            imags.append(real * sine + imag * cosine)
        real = jnp.concatenate(reals, axis=0)
        imag = jnp.concatenate(imags, axis=0)
        rows_real.append(jnp.concatenate([real, -imag], axis=1))
        rows_real.append(jnp.concatenate([imag, real], axis=1))
    rows = jnp.concatenate(rows_real, axis=0)
    spectrum = dot3((wide_high[...], wide_low[...]), split_value(rows), ((1,), (1,)))
    lane = lax.broadcasted_iota(jnp.int32, (8, LANES), 1)
    table = jnp.zeros((8, LANES), f32)
    for i in range(16):
        for limb in range(2):
            table = jnp.where(lane == 2 * i + limb, keep[i, limb], table)
            table = jnp.where(lane == 32 + 2 * i + limb, scale[i, limb], table)
    for pair in range(2):
        out[pl.ds(pair * 256, LANES, stride=2), :] = spectrum[:, pair * LANES : (pair + 1) * LANES]
    for tile in range(ROOTS // 8):
        out[pl.ds(tile * 16 + 1, 8, stride=2), :] = table


def complex_scale(value, cosine, sine):
    real, imag = value
    return real * cosine - imag * sine, real * sine + imag * cosine


def split_ring(values, theta):
    if len(values) == 1:
        return [(theta, values[0])]
    half = len(values) // 2
    cosine, sine = math.cos(theta / 2), math.sin(theta / 2)
    left, right = [], []
    for low, high in zip(values[:half], values[half:]):
        moved = complex_scale(high, cosine, sine)
        left.append((low[0] + moved[0], low[1] + moved[1]))
        right.append((low[0] - moved[0], low[1] - moved[1]))
    return split_ring(left, theta / 2) + split_ring(right, theta / 2 + math.pi)


def join_ring(values, theta):
    if len(values) == 1:
        return values
    half = len(values) // 2
    left = join_ring(values[:half], theta / 2)
    right = join_ring(values[half:], theta / 2 + math.pi)
    cosine, sine = math.cos(theta / 2), math.sin(theta / 2)
    low, high = [], []
    for one, two in zip(left, right):
        low.append((one[0] + two[0], one[1] + two[1]))
        high.append(complex_scale((one[0] - two[0], one[1] - two[1]), cosine, -sine))
    return low + high


def root_angles(count, theta):
    if count == 1:
        return [theta]
    return root_angles(count // 2, theta / 2) + root_angles(count // 2, theta / 2 + math.pi)


def tensor_kernel(spread, to_special, out, real_held, imag_held, table_held, table, table_sem):
    table_held[...] = spread[pl.ds(1, GROUPS, stride=2 * COEF), :]
    copy = pltpu.make_async_copy(table_held, table, table_sem)
    copy.start()
    lane = lax.broadcasted_iota(jnp.int32, (8, LANES), 1)
    half = lane < 64
    sign = jnp.where(half, 1.0, -1.0).astype(f32)
    limb_low = (lane & 4) == 0
    comp = lane & 3

    def roll(value, shift):
        return pltpu.roll(value, shift % LANES, 1)

    packed = []
    for e in range(COEF // 2):
        even = spread[pl.ds(4 * e, GROUPS, stride=2 * COEF), :]
        odd = spread[pl.ds(4 * e + 2, GROUPS, stride=2 * COEF), :]
        packed.append((jnp.where(half, even, roll(odd, 64)), jnp.where(half, roll(even, 64), odd)))
    for place, (theta, (real, imag)) in enumerate(split_ring(packed, math.pi)):
        cosine = sign * math.cos(theta / 2)
        sine = sign * math.sin(theta / 2)
        real_other, imag_other = roll(real, 64), roll(imag, 64)
        real_low, imag_low = jnp.where(half, real, real_other), jnp.where(half, imag, imag_other)
        real_high, imag_high = jnp.where(half, real_other, real), jnp.where(half, imag_other, imag)
        real_held[place * 8 : place * 8 + 8, :] = real_low + (cosine * real_high - sine * imag_high)
        imag_held[place * 8 : place * 8 + 8, :] = imag_low + (cosine * imag_high + sine * real_high)

    limbs = []
    for group in range(GROUPS):
        pair = []
        for ref in (real_held, imag_held):
            one = ref[pl.ds(group, 8, stride=8), :]
            two = ref[pl.ds(64 + group, 8, stride=8), :]
            pair.append((jnp.where(limb_low, one, roll(two, 4)), jnp.where(limb_low, roll(one, -4), two)))
        limbs.append((pair[0][0], pair[1][0]))
        limbs.append((pair[0][1], pair[1][1]))

    def tensor(value):
        left, right = [], []
        for part in value:
            after = roll(part, -1)
            left.append(jnp.where(comp == 1, after, jnp.where(comp == 3, roll(part, 3), part)))
            right.append(jnp.where((comp & 1) == 0, after, part))
        return (
            left[0] * right[0] - left[1] * right[1],
            left[0] * right[1] + left[1] * right[0],
        )

    copy.wait()
    totals = [None] * 16
    for q in range(32):
        if q < 16:
            value = limbs[q]
        else:
            real = imag = None
            for s in range(16):
                weight = to_special[q - 16, s]
                term_real, term_imag = weight * limbs[s][0], weight * limbs[s][1]
                real = term_real if real is None else real + term_real
                imag = term_imag if imag is None else imag + term_imag
            value = (real, imag)
        product = tensor(value)
        group, place = (q % 16) // 2, (q % 2) + (0 if q < 16 else 32)
        for i in range(16):
            weight = table[group, place + 2 * i]
            term = (weight * product[0], weight * product[1])
            totals[i] = term if totals[i] is None else (totals[i][0] + term[0], totals[i][1] + term[1])

    for group in range(GROUPS):
        for part, ref in enumerate((real_held, imag_held)):
            low, high = totals[2 * group][part], totals[2 * group + 1][part]
            ref[pl.ds(group, 8, stride=8), :] = jnp.where(limb_low, low, roll(high, 4))
            ref[pl.ds(64 + group, 8, stride=8), :] = jnp.where(limb_low, roll(low, -4), high)

    share = 1.0 / (COEF * BLOCK)
    joined = []
    for place, theta in enumerate(root_angles(COEF // 2, math.pi)):
        real = real_held[place * 8 : place * 8 + 8, :]
        imag = imag_held[place * 8 : place * 8 + 8, :]
        real_other, imag_other = roll(real, 64), roll(imag, 64)
        root = complex(math.cos(theta / 2), math.sin(theta / 2))
        plus, minus = (1 - 1j * root) * share, (1 + 1j * root) * share
        own = (plus, -root.conjugate() * minus)
        other = (minus, root.conjugate() * plus)
        own_real, own_imag = jnp.where(half, own[0].real, own[1].real), jnp.where(half, own[0].imag, own[1].imag)
        other_real = jnp.where(half, other[0].real, other[1].real)
        other_imag = jnp.where(half, other[0].imag, other[1].imag)
        joined.append(
            (
                (own_real * real - own_imag * imag) + (other_real * real_other - other_imag * imag_other),
                (own_real * imag + own_imag * real) + (other_real * imag_other + other_imag * real_other),
            )
        )
    for e, (real, imag) in enumerate(join_ring(joined, math.pi)):
        out[pl.ds(2 * e, GROUPS, stride=COEF), :] = jnp.where(half, real, roll(imag, 64))
        out[pl.ds(2 * e + 1, GROUPS, stride=COEF), :] = jnp.where(half, roll(real, 64), imag)


def restore_kernel(gathered, wide_high, wide_low, twiddle, out):
    row = lax.broadcasted_iota(jnp.int32, (8, LANES), 0)
    middle = (row & 3) == 1
    wide = (wide_high[...], wide_low[...])
    for pair in range(2):
        values = gathered[pair * LANES : (pair + 1) * LANES, :]
        spun = dot3(split_value(values), wide, ((0,), (0,)))
        real = spun[:64, :LANES] + spun[64:, LANES:]
        imag = spun[64:, :LANES] - spun[:64, LANES:]
        turned = []
        for k0 in range(K0):
            cosine = twiddle[k0 : k0 + 1, :]
            sine = twiddle[K0 + k0 : K0 + k0 + 1, :]
            own_real, own_imag = real[k0 * 8 : k0 * 8 + 8], imag[k0 * 8 : k0 * 8 + 8]
            turned.append((own_real * cosine + own_imag * sine, own_imag * cosine - own_real * sine))
        halves = []
        for k0 in range(K0 // 2):
            one, two = turned[k0], turned[k0 + K0 // 2]
            halves.append(((one[0] + two[0], one[1] + two[1]), (one[0] - two[0], one[1] - two[1])))
        for u in range(U):
            total = None
            for k0 in range(K0 // 2):
                cosine, sine = turn(u, k0)
                real_part, imag_part = halves[k0][u % 2]
                term = real_part if u == 0 else real_part * cosine + imag_part * sine
                total = term if total is None else total + term
            total = jnp.where(middle, total + pltpu.roll(total, 6, 0), total)
            for limb in range(2):
                out[limb, pair, :, u * LANES : (u + 1) * LANES] = total[limb * 4 : limb * 4 + 3]


def in_vmem():
    return pl.BlockSpec(memory_space=pltpu.VMEM)


def in_smem():
    return pl.BlockSpec(memory_space=pltpu.SMEM)


def per_device(first_cipher, second_cipher, to_special, keep_table, scale_table):
    (wide_high, wide_low), twiddle = turn_tables()
    wide_high, wide_low, twiddle = jnp.asarray(wide_high), jnp.asarray(wide_low), jnp.asarray(twiddle)
    params = pltpu.CompilerParams(vmem_limit_bytes=32 * 1024 * 1024)
    spectra = pl.pallas_call(
        evaluate_kernel,
        out_shape=jax.ShapeDtypeStruct((2 * ROOTS, LANES), f32),
        in_specs=[in_vmem()] * 2 + [in_smem()] * 2 + [in_vmem()] * 3,
        out_specs=in_vmem(),
        scratch_shapes=[pltpu.VMEM((2 * U * 8, LANES), f32)],
        compiler_params=params,
        name="evaluate",
    )(first_cipher, second_cipher, keep_table, scale_table, wide_high, wide_low, twiddle)
    spread = lax.all_to_all(spectra.reshape(ROOTS, 2, LANES), ("limb", "coef"), 0, 0)
    scaled = pl.pallas_call(
        tensor_kernel,
        out_shape=jax.ShapeDtypeStruct((ROOTS, LANES), f32),
        in_specs=[in_vmem(), in_smem()],
        out_specs=in_vmem(),
        scratch_shapes=[
            pltpu.VMEM((LANES, LANES), f32),
            pltpu.VMEM((LANES, LANES), f32),
            pltpu.VMEM((8, LANES), f32),
            pltpu.SMEM((8, LANES), f32),
            pltpu.SemaphoreType.DMA,
        ],
        compiler_params=params,
        name="tensor",
    )(spread.reshape(2 * ROOTS, LANES), to_special)
    gathered = lax.all_to_all(scaled.reshape(ROOTS, 1, LANES), ("limb", "coef"), 0, 0)
    return pl.pallas_call(
        restore_kernel,
        out_shape=jax.ShapeDtypeStruct((2, 2, 3, BLOCK), f32),
        in_specs=[in_vmem()] * 4,
        out_specs=in_vmem(),
        compiler_params=params,
        name="restore",
    )(gathered.reshape(ROOTS, LANES), wide_high, wide_low, twiddle)


def solution(mesh):
    return jax.shard_map(
        per_device,
        mesh=mesh,
        in_specs=(
            P("limb", None, None, "coef"),
            P("limb", None, None, "coef"),
            P(),
            P(None, "limb"),
            P(None, "limb"),
        ),
        out_specs=P("limb", None, None, "coef"),
        check_vma=False,
    )
```

time: 382 us -> 58 us (0.15)
  the two profiles are of different devices: /device:TPU:2 before, /device:TPU:1 now
where the time goes in v1:
time: 58 us; the launch traced here: 57.5 us
  blocking collectives  48.8 us (84%)
  local copies, waits for them, and re-layouts  4.75 us (8%)
  Pallas kernels  3.92 us (7%)
    all_to_all x1, blocking collectives, per_device(): lax.all_to_all(spectra.reshape(ROOTS, 2, LANES), ('limb', 'coef'), 0, 0)  31 us
    all_to_all x1, blocking collectives, per_device(): lax.all_to_all(scaled.reshape(ROOTS, 1, LANES), ('limb', 'coef'), 0, 0)  17.8 us
    unnamed x20, local copies, waits for them, and re-layouts  4.09 us
    pallas_call x1, Pallas kernels, per_device(): pl.pallas_call(tensor_kernel, out_shape=jax.ShapeDtypeStruct((ROOTS, LANE...  2.46 us

profile of v1, /device:TPU:1, one launch (start us, length us, event | category | flops | bytes accessed | tf_op | source)
XLA Modules:
  0.0 57.5 jit_solution(14225554004706391217)
XLA Ops:
  0.0 0.0 copy-start.4
  0.0 0.0 copy-start.8
  0.0 0.8 %copy.12.keep = f32[16,2]{1,0:T(8,128)S(1)} copy(f32[16,2]{0,1:T(2,128)} %param.11) | data formatting | bytes 256 | tf_op args[3]
  0.8 0.0 copy-done.8
  0.8 0.1 copy.13.scale
  0.9 0.0 copy-done.4
  0.9 0.0 copy-start
  0.9 0.8 %copy-done = bf16[128,256]{1,0:T(8,128)(2,1)S(1)} copy-done((bf16[128,256]{1,0:T(8,128)(2,1)S(1)}, bf16[128,256]{1,0:T(8,128)(2,1)}, u32[]{:S(2)}) %copy-start) | copy-done | bytes 65560
  1.7 0.0 copy-start.2
  1.7 0.8 %copy-done.2 = bf16[128,256]{1,0:T(8,128)(2,1)S(1)} copy-done((bf16[128,256]{1,0:T(8,128)(2,1)S(1)}, bf16[128,256]{1,0:T(8,128)(2,1)}, u32[]{:S(2)}) %copy-start.2) | copy-done | bytes 65560
  2.6 0.0 copy-start.5
  2.6 0.8 %copy-done.5 = f32[2,2,2,1024]{3,2,1,0:T(2,128)S(1)} copy-done((f32[2,2,2,1024]{3,2,1,0:T(2,128)S(1)}, f32[2,2,2,1024]{3,2,1,0:T(2,128)}, u32[]{:S(2)}) %copy-start.5) | copy-done | bytes 32792
  3.3 0.0 copy-start.6
  3.3 0.8 %copy-done.6 = f32[2,2,2,1024]{3,2,1,0:T(2,128)S(1)} copy-done((f32[2,2,2,1024]{3,2,1,0:T(2,128)S(1)}, f32[2,2,2,1024]{3,2,1,0:T(2,128)}, u32[]{:S(2)}) %copy-start.6) | copy-done | bytes 32792
  4.1 1.1 %evaluate.1 = f32[512,128]{1,0:T(8,128)S(1)} custom-call(f32[2,2,2,1024]{3,2,1,0:T(2,128)S(1)} %copy-done.5, f32[2,2,2,1024]{3,2,1,0:T(2,128)S(1)} %copy-done.6, f32[16,2]{1,0:T(8,128)S(1)} %copy.12.keep, f32[16,2]{1,0:T(8,128)S(1)} %copy.13.scale, bf16[128,256]{1,0:T(8,128)(2,1)S(1)} %copy-done.2, bf16[128,256]{1,0:T(8,128)(2,1)S(1)} %copy-done, ...), custom_call_target="tpu_custom_call" | custom-call | tf_op jit(solution)/shard_map/evaluate/pallas_call | solution.py:290
  5.2 0.0 copy-start.7
  5.2 31.0 %all_to_all.10 = f32[256,2,128]{2,1,0:T(2,128)S(1)} all-to-all(f32[256,2,128]{2,1,0:T(2,128)S(1)} %bitcast.7), channel_id=1, replica_groups=mesh['limb'=8,'coef'=32] {'limb','coef'}, dimensions={0} | all-to-all | bytes 524288 | tf_op jit(solution)/shard_map/all_to_all | solution.py:299
  36.2 0.0 copy-done.7
  36.2 2.5 %tensor.1 = f32[256,128]{1,0:T(8,128)S(1)} custom-call(f32[512,128]{1,0:T(8,128)S(1)} %bitcast.6, f32[16,16]{1,0:T(8,128)S(1)} %copy-done.7), custom_call_target="tpu_custom_call" | custom-call | tf_op jit(solution)/shard_map/tensor/pallas_call | solution.py:300
  38.6 0.0 copy-start.1
  38.7 0.0 copy-start.3
  38.7 17.8 %all_to_all.11 = f32[256,1,128]{2,1,0:T(1,128)S(1)} all-to-all(f32[256,1,128]{2,1,0:T(1,128)S(1)} %bitcast.8), channel_id=1, replica_groups=mesh['limb'=8,'coef'=32] {'limb','coef'}, dimensions={0} | all-to-all | bytes 262144 | tf_op jit(solution)/shard_map/all_to_all | solution.py:315
  56.5 0.0 copy-done.1
  56.5 0.0 copy-done.3
  56.5 0.3 restore.1
  56.8 0.7 %copy.15 = f32[2,2,3,1024]{3,1,2,0:T(2,128)} copy(f32[2,2,3,1024]{3,2,1,0:T(4,128)S(1)} %restore.1) | data formatting | bytes 98304 | tf_op jit(solution)/shard_map/restore/pallas_call | solution.py:316
Async XLA Ops:
  0.0 0.9 %copy-start.4 = (f32[16,128]{1,0:T(8,128)S(1)}, f32[16,128]{1,0:T(8,128)}, u32[]{:S(2)}) copy-start(f32[16,128]{1,0:T(8,128)} %constant.8.clone.twiddle) | copy-start | bytes 24580
  0.0 0.8 %copy-start.8 = (f32[16,2]{0,1:T(2,128)S(1)}, f32[16,2]{0,1:T(2,128)}, u32[]{:S(2)}) copy-start(f32[16,2]{0,1:T(2,128)} %param.12) | copy-start | bytes 388
  0.9 0.8 %copy-start = (bf16[128,256]{1,0:T(8,128)(2,1)S(1)}, bf16[128,256]{1,0:T(8,128)(2,1)}, u32[]{:S(2)}) copy-start(bf16[128,256]{1,0:T(8,128)(2,1)} %constant.7.clone.wide_low) | copy-start | bytes 196612
  1.7 0.8 %copy-start.2 = (bf16[128,256]{1,0:T(8,128)(2,1)S(1)}, bf16[128,256]{1,0:T(8,128)(2,1)}, u32[]{:S(2)}) copy-start(bf16[128,256]{1,0:T(8,128)(2,1)} %constant.6.clone.wide_high) | copy-start | bytes 196612
  2.6 0.8 %copy-start.5 = (f32[2,2,2,1024]{3,2,1,0:T(2,128)S(1)}, f32[2,2,2,1024]{3,2,1,0:T(2,128)}, u32[]{:S(2)}) copy-start(f32[2,2,2,1024]{3,2,1,0:T(2,128)} %first.1) | copy-start | bytes 98308
  3.3 0.8 %copy-start.6 = (f32[2,2,2,1024]{3,2,1,0:T(2,128)S(1)}, f32[2,2,2,1024]{3,2,1,0:T(2,128)}, u32[]{:S(2)}) copy-start(f32[2,2,2,1024]{3,2,1,0:T(2,128)} %second.1) | copy-start | bytes 98308
  5.2 31.0 %copy-start.7 = (f32[16,16]{1,0:T(8,128)S(1)}, f32[16,16]{1,0:T(8,128)}, u32[]{:S(2)}) copy-start(f32[16,16]{1,0:T(8,128)} %to_special.1) | copy-start | bytes 3076
  38.6 17.9 %copy-start.1 = (bf16[128,256]{1,0:T(8,128)(2,1)S(1)}, bf16[128,256]{1,0:T(8,128)(2,1)}, u32[]{:S(2)}) copy-start(bf16[128,256]{1,0:T(8,128)(2,1)} %constant.7.clone.wide_low) | copy-start | bytes 196612
  38.7 17.8 %copy-start.3 = (bf16[128,256]{1,0:T(8,128)(2,1)S(1)}, bf16[128,256]{1,0:T(8,128)(2,1)}, u32[]{:S(2)}) copy-start(bf16[128,256]{1,0:T(8,128)(2,1)} %constant.6.clone.wide_high) | copy-start | bytes 196612

commit v2 on v1

--- a/solution.py
+++ b/solution.py
@@ -55,7 +55,29 @@
     return math.cos(angle), math.sin(angle)
 
 
-def evaluate_kernel(first, second, keep, scale, wide_high, wide_low, twiddle, out, held):
+def evaluate_kernel(
+    first_far, second_far, keep_far, scale_far, high_far, low_far, twiddle_far,
+    out,
+    first, second, keep, scale, wide_high, wide_low, twiddle, held, sems,
+):
+    copies = [
+        pltpu.make_async_copy(far, near, sems.at[place])
+        for place, (far, near) in enumerate(
+            (
+                (first_far, first),
+                (second_far, second),
+                (twiddle_far, twiddle),
+                (high_far, wide_high),
+                (low_far, wide_low),
+                (keep_far, keep),
+                (scale_far, scale),
+            )
+        )
+    ]
+    for copy in copies:
+        copy.start()
+    copies[0].wait()
+    copies[1].wait()
     for pair in range(2):
         for u in range(U):
             base = (pair * U + u) * 8
@@ -64,7 +86,8 @@
                     held[pl.ds(base + limb * 4 + cipher, 2, stride=2), :] = ref[
                         limb, pair, :, u * LANES : (u + 1) * LANES
                     ]
-    rows_real = []
+    copies[2].wait()
+    blocks = []
     for pair in range(2):
         parts = [held[(pair * U + u) * 8 : (pair * U + u + 1) * 8, :] for u in range(U)]
         spun = [None] * K0
@@ -92,16 +115,21 @@
             imags.append(real * sine + imag * cosine)
         real = jnp.concatenate(reals, axis=0)
         imag = jnp.concatenate(imags, axis=0)
-        rows_real.append(jnp.concatenate([real, -imag], axis=1))
-        rows_real.append(jnp.concatenate([imag, real], axis=1))
-    rows = jnp.concatenate(rows_real, axis=0)
+        blocks.append(jnp.concatenate([real, -imag], axis=1))
+        blocks.append(jnp.concatenate([imag, real], axis=1))
+    rows = jnp.concatenate(blocks, axis=0)
+    copies[3].wait()
+    copies[4].wait()
     spectrum = dot3((wide_high[...], wide_low[...]), split_value(rows), ((1,), (1,)))
+    copies[5].wait()
+    copies[6].wait()
     lane = lax.broadcasted_iota(jnp.int32, (8, LANES), 1)
     table = jnp.zeros((8, LANES), f32)
     for i in range(16):
         for limb in range(2):
-            table = jnp.where(lane == 2 * i + limb, keep[i, limb], table)
-            table = jnp.where(lane == 32 + 2 * i + limb, scale[i, limb], table)
+            place = limb * 16 + (i % 2) * 8 + i // 2
+            table = jnp.where(lane == place, keep[limb, i], table)
+            table = jnp.where(lane == 32 + place, scale[limb, i], table)
     for pair in range(2):
         out[pl.ds(pair * 256, LANES, stride=2), :] = spectrum[:, pair * LANES : (pair + 1) * LANES]
     for tile in range(ROOTS // 8):
@@ -146,42 +174,56 @@
     return root_angles(count // 2, theta / 2) + root_angles(count // 2, theta / 2 + math.pi)
 
 
-def tensor_kernel(spread, to_special, out, real_held, imag_held, table_held, table, table_sem):
-    table_held[...] = spread[pl.ds(1, GROUPS, stride=2 * COEF), :]
-    copy = pltpu.make_async_copy(table_held, table, table_sem)
-    copy.start()
+def mix(weights, values, dims):
+    high, low = split_value(values)
+    axis = dims[0][0]
+    left = jnp.concatenate([weights[0], weights[0], weights[1]], axis=axis)
+    return lax.dot_general(
+        left, jnp.concatenate([high, low, high], axis=0), (dims, ((), ())), preferred_element_type=f32
+    )
+
+
+def tensor_kernel(spread, to_special, out):
     lane = lax.broadcasted_iota(jnp.int32, (8, LANES), 1)
     half = lane < 64
     sign = jnp.where(half, 1.0, -1.0).astype(f32)
     limb_low = (lane & 4) == 0
-    comp = lane & 3
+    comp = lax.broadcasted_iota(jnp.int32, (16, LANES), 1) & 3
 
     def roll(value, shift):
         return pltpu.roll(value, shift % LANES, 1)
+
+    rows = jnp.concatenate([to_special[pl.ds(limb, 8, stride=2), :] for limb in range(2)], axis=0)
+    old = lax.broadcasted_iota(jnp.int32, (16, 16), 0)
+    new = lax.broadcasted_iota(jnp.int32, (16, 16), 1)
+    order = jnp.where(old == 2 * (new & 7) + (new >> 3), 1.0, 0.0).astype(bf16)
+    extend = split_value(
+        sum(
+            lax.dot_general(part, order, (((1,), (0,)), ((), ())), preferred_element_type=f32)
+            for part in split_value(rows)
+        )
+    )
+    table = spread[pl.ds(1, GROUPS, stride=2 * COEF), :]
+    shrink = split_value(jnp.concatenate([table[:, 16 * j : 16 * j + 16] for j in range(4)], axis=0))
 
     packed = []
     for e in range(COEF // 2):
         even = spread[pl.ds(4 * e, GROUPS, stride=2 * COEF), :]
         odd = spread[pl.ds(4 * e + 2, GROUPS, stride=2 * COEF), :]
         packed.append((jnp.where(half, even, roll(odd, 64)), jnp.where(half, roll(even, 64), odd)))
-    for place, (theta, (real, imag)) in enumerate(split_ring(packed, math.pi)):
+    spectra = []
+    for theta, (real, imag) in split_ring(packed, math.pi):
         cosine = sign * math.cos(theta / 2)
         sine = sign * math.sin(theta / 2)
         real_other, imag_other = roll(real, 64), roll(imag, 64)
         real_low, imag_low = jnp.where(half, real, real_other), jnp.where(half, imag, imag_other)
         real_high, imag_high = jnp.where(half, real_other, real), jnp.where(half, imag_other, imag)
-        real_held[place * 8 : place * 8 + 8, :] = real_low + (cosine * real_high - sine * imag_high)
-        imag_held[place * 8 : place * 8 + 8, :] = imag_low + (cosine * imag_high + sine * real_high)
-
-    limbs = []
-    for group in range(GROUPS):
-        pair = []
-        for ref in (real_held, imag_held):
-            one = ref[pl.ds(group, 8, stride=8), :]
-            two = ref[pl.ds(64 + group, 8, stride=8), :]
-            pair.append((jnp.where(limb_low, one, roll(two, 4)), jnp.where(limb_low, roll(one, -4), two)))
-        limbs.append((pair[0][0], pair[1][0]))
-        limbs.append((pair[0][1], pair[1][1]))
+        spectra.append(
+            (
+                real_low + (cosine * real_high - sine * imag_high),
+                imag_low + (cosine * imag_high + sine * real_high),
+            )
+        )
 
     def tensor(value):
         left, right = [], []
@@ -194,37 +236,34 @@
             left[0] * right[1] + left[1] * right[0],
         )
 
-    copy.wait()
-    totals = [None] * 16
-    for q in range(32):
-        if q < 16:
-            value = limbs[q]
-        else:
-            real = imag = None
-            for s in range(16):
-                weight = to_special[q - 16, s]
-                term_real, term_imag = weight * limbs[s][0], weight * limbs[s][1]
-                real = term_real if real is None else real + term_real
-                imag = term_imag if imag is None else imag + term_imag
-            value = (real, imag)
-        product = tensor(value)
-        group, place = (q % 16) // 2, (q % 2) + (0 if q < 16 else 32)
-        for i in range(16):
-            weight = table[group, place + 2 * i]
-            term = (weight * product[0], weight * product[1])
-            totals[i] = term if totals[i] is None else (totals[i][0] + term[0], totals[i][1] + term[1])
-
-    for group in range(GROUPS):
-        for part, ref in enumerate((real_held, imag_held)):
-            low, high = totals[2 * group][part], totals[2 * group + 1][part]
-            ref[pl.ds(group, 8, stride=8), :] = jnp.where(limb_low, low, roll(high, 4))
-            ref[pl.ds(64 + group, 8, stride=8), :] = jnp.where(limb_low, roll(low, -4), high)
+    mixed = []
+    for place in range(COEF // 4):
+        own = []
+        for part in range(2):
+            one, two = spectra[2 * place][part], spectra[2 * place + 1][part]
+            own.append(
+                jnp.concatenate(
+                    [jnp.where(limb_low, one, roll(two, 4)), jnp.where(limb_low, roll(one, -4), two)], axis=0
+                )
+            )
+        special = mix(extend, jnp.concatenate(own, axis=1), ((1,), (0,)))
+        own = tensor(own)
+        special = tensor((special[:, :LANES], special[:, LANES:]))
+        products = jnp.concatenate(
+            [jnp.concatenate(own, axis=1), jnp.concatenate(special, axis=1)], axis=0
+        )
+        scaled = mix(shrink, products, ((0,), (0,)))
+        parts = []
+        for part in range(2):
+            both = scaled[:, part * LANES : (part + 1) * LANES]
+            low, high = both[:8], both[8:]
+            parts.append((jnp.where(limb_low, low, roll(high, 4)), jnp.where(limb_low, roll(low, -4), high)))
+        mixed.append((parts[0][0], parts[1][0]))
+        mixed.append((parts[0][1], parts[1][1]))
 
     share = 1.0 / (COEF * BLOCK)
     joined = []
-    for place, theta in enumerate(root_angles(COEF // 2, math.pi)):
-        real = real_held[place * 8 : place * 8 + 8, :]
-        imag = imag_held[place * 8 : place * 8 + 8, :]
+    for (real, imag), theta in zip(mixed, root_angles(COEF // 2, math.pi)):
         real_other, imag_other = roll(real, 64), roll(imag, 64)
         root = complex(math.cos(theta / 2), math.sin(theta / 2))
         plus, minus = (1 - 1j * root) * share, (1 + 1j * root) * share
@@ -272,15 +311,21 @@
                 total = term if total is None else total + term
             total = jnp.where(middle, total + pltpu.roll(total, 6, 0), total)
             for limb in range(2):
-                out[limb, pair, :, u * LANES : (u + 1) * LANES] = total[limb * 4 : limb * 4 + 3]
+                for part in range(3):
+                    row = limb * 4 + part
+                    out[limb, part, pair : pair + 1, u * LANES : (u + 1) * LANES] = total[row : row + 1]
 
 
 def in_vmem():
     return pl.BlockSpec(memory_space=pltpu.VMEM)
 
 
-def in_smem():
-    return pl.BlockSpec(memory_space=pltpu.SMEM)
+def in_hbm():
+    return pl.BlockSpec(memory_space=pltpu.HBM)
+
+
+def kept_far(*arrays):
+    return [pltpu.with_memory_space_constraint(array, pltpu.HBM) for array in arrays]
 
 
 def per_device(first_cipher, second_cipher, to_special, keep_table, scale_table):
@@ -290,37 +335,41 @@
     spectra = pl.pallas_call(
         evaluate_kernel,
         out_shape=jax.ShapeDtypeStruct((2 * ROOTS, LANES), f32),
-        in_specs=[in_vmem()] * 2 + [in_smem()] * 2 + [in_vmem()] * 3,
+        in_specs=[in_hbm()] * 7,
         out_specs=in_vmem(),
-        scratch_shapes=[pltpu.VMEM((2 * U * 8, LANES), f32)],
+        scratch_shapes=[
+            pltpu.VMEM(first_cipher.shape, f32),
+            pltpu.VMEM(second_cipher.shape, f32),
+            pltpu.SMEM((2, 16), f32),
+            pltpu.SMEM((2, 16), f32),
+            pltpu.VMEM(wide_high.shape, bf16),
+            pltpu.VMEM(wide_low.shape, bf16),
+            pltpu.VMEM(twiddle.shape, f32),
+            pltpu.VMEM((2 * U * 8, LANES), f32),
+            pltpu.SemaphoreType.DMA((7,)),
+        ],
         compiler_params=params,
         name="evaluate",
-    )(first_cipher, second_cipher, keep_table, scale_table, wide_high, wide_low, twiddle)
+    )(*kept_far(first_cipher, second_cipher, keep_table.T, scale_table.T, wide_high, wide_low, twiddle))
     spread = lax.all_to_all(spectra.reshape(ROOTS, 2, LANES), ("limb", "coef"), 0, 0)
     scaled = pl.pallas_call(
         tensor_kernel,
         out_shape=jax.ShapeDtypeStruct((ROOTS, LANES), f32),
-        in_specs=[in_vmem(), in_smem()],
+        in_specs=[in_vmem()] * 2,
         out_specs=in_vmem(),
-        scratch_shapes=[
-            pltpu.VMEM((LANES, LANES), f32),
-            pltpu.VMEM((LANES, LANES), f32),
-            pltpu.VMEM((8, LANES), f32),
-            pltpu.SMEM((8, LANES), f32),
-            pltpu.SemaphoreType.DMA,
-        ],
         compiler_params=params,
         name="tensor",
     )(spread.reshape(2 * ROOTS, LANES), to_special)
     gathered = lax.all_to_all(scaled.reshape(ROOTS, 1, LANES), ("limb", "coef"), 0, 0)
-    return pl.pallas_call(
+    product = pl.pallas_call(
         restore_kernel,
-        out_shape=jax.ShapeDtypeStruct((2, 2, 3, BLOCK), f32),
+        out_shape=jax.ShapeDtypeStruct((2, 3, 2, BLOCK), f32),
         in_specs=[in_vmem()] * 4,
         out_specs=in_vmem(),
         compiler_params=params,
         name="restore",
     )(gathered.reshape(ROOTS, LANES), wide_high, wide_low, twiddle)
+    return product.transpose(0, 2, 1, 3)
 
 
 def solution(mesh):

time: 58 us -> 53 us (0.914)
  local copies, waits for them, and re-layouts: 4.75 us -> 0.03 us
    unnamed x20 -> x8, local copies, waits for them, and re-layouts: 4.09 us -> 0.03 us
    pallas_call x1, Pallas kernels: 2.46 us -> 1.54 us  [per_device(): pl.pallas_call(tensor_kernel, out_shape=jax.ShapeDtypeStruct((ROOTS, LANE...]
    pallas_call x1 -> x0, local copies, waits for them, and re-layouts: 0.66 us -> none  [per_device(): pl.pallas_call(restore_kernel, out_shape=jax.ShapeDtypeStruct((2, 2, 3, B...]
    pallas_call x1, Pallas kernels: 0.34 us -> 0.98 us  [per_device(): pl.pallas_call(restore_kernel, out_shape=jax.ShapeDtypeStruct((2, 3, 2, B...]
where the time goes in v2:
time: 53 us; the launch traced here: 52.7 us
  blocking collectives  48.8 us (92%)
  Pallas kernels  3.85 us (7%)
    all_to_all x1, blocking collectives, per_device(): lax.all_to_all(spectra.reshape(ROOTS, 2, LANES), ('limb', 'coef'), 0, 0)  31 us
    all_to_all x1, blocking collectives, per_device(): lax.all_to_all(scaled.reshape(ROOTS, 1, LANES), ('limb', 'coef'), 0, 0)  17.8 us
    pallas_call x1, Pallas kernels, per_device(): pl.pallas_call(tensor_kernel, out_shape=jax.ShapeDtypeStruct((ROOTS, LANE...  1.54 us
    pallas_call x1, Pallas kernels, per_device(): pl.pallas_call(evaluate_kernel, out_shape=jax.ShapeDtypeStruct((2 * ROOTS...  1.34 us

profile of v2, /device:TPU:1, one launch (start us, length us, event | category | flops | bytes accessed | tf_op | source)
XLA Modules:
  0.0 52.7 jit_solution(11224600551781853679)
XLA Ops:
  0.0 1.3 %evaluate.1 = f32[512,128]{1,0:T(8,128)S(1)} custom-call(f32[2,2,2,1024]{3,2,1,0:T(2,128)} %first_far.1, f32[2,2,2,1024]{3,2,1,0:T(2,128)} %second_far.1, f32[2,16]{1,0:T(2,128)} %bitcast.13, f32[2,16]{1,0:T(2,128)} %bitcast.14, bf16[128,256]{1,0:T(8,128)(2,1)} %constant.6.clone.high_far.wide_high, bf16[128,256]{1,0:T(8,128)(2,1)} %constant.7.clone.low_far.wide_low, ...), custom_call_target="tpu_custom_call" | custom-call | tf_op jit(solution)/shard_map/evaluate/pallas_call | solution.py:335
  1.3 0.0 copy-start.3
  1.4 31.0 %all_to_all.10 = f32[256,2,128]{2,1,0:T(2,128)S(1)} all-to-all(f32[256,2,128]{2,1,0:T(2,128)S(1)} %bitcast.9), channel_id=1, replica_groups=mesh['limb'=8,'coef'=32] {'limb','coef'}, dimensions={0} | all-to-all | bytes 524288 | tf_op jit(solution)/shard_map/all_to_all | solution.py:354
  32.3 0.0 copy-done.3
  32.3 1.5 %tensor.1 = f32[256,128]{1,0:T(8,128)S(1)} custom-call(f32[512,128]{1,0:T(8,128)S(1)} %bitcast.10, f32[16,16]{1,0:T(8,128)S(1)} %copy-done.3), custom_call_target="tpu_custom_call" | custom-call | tf_op jit(solution)/shard_map/tensor/pallas_call | solution.py:355
  33.9 0.0 copy-start
  33.9 0.0 copy-start.1
  33.9 0.0 copy-start.2
  33.9 17.8 %all_to_all.11 = f32[256,1,128]{2,1,0:T(1,128)S(1)} all-to-all(f32[256,1,128]{2,1,0:T(1,128)S(1)} %bitcast.11), channel_id=1, replica_groups=mesh['limb'=8,'coef'=32] {'limb','coef'}, dimensions={0} | all-to-all | bytes 262144 | tf_op jit(solution)/shard_map/all_to_all | solution.py:363
  51.7 0.0 copy-done
  51.7 0.0 copy-done.1
  51.7 0.0 copy-done.2
  51.7 1.0 %restore.1 = f32[2,3,2,1024]{3,2,1,0:T(2,128)} custom-call(f32[256,128]{1,0:T(8,128)S(1)} %bitcast.12, bf16[128,256]{1,0:T(8,128)(2,1)S(1)} %copy-done.1, bf16[128,256]{1,0:T(8,128)(2,1)S(1)} %copy-done, f32[16,128]{1,0:T(8,128)S(1)} %copy-done.2), custom_call_target="tpu_custom_call" | custom-call | tf_op jit(solution)/shard_map/restore/pallas_call | solution.py:364
Async XLA Ops:
  1.3 31.0 %copy-start.3 = (f32[16,16]{1,0:T(8,128)S(1)}, f32[16,16]{1,0:T(8,128)}, u32[]{:S(2)}) copy-start(f32[16,16]{1,0:T(8,128)} %to_special.1) | copy-start | bytes 3076
  33.9 17.9 %copy-start = (bf16[128,256]{1,0:T(8,128)(2,1)S(1)}, bf16[128,256]{1,0:T(8,128)(2,1)}, u32[]{:S(2)}) copy-start(bf16[128,256]{1,0:T(8,128)(2,1)} %constant.7.clone.low_far.wide_low) | copy-start | bytes 196612
  33.9 17.9 %copy-start.1 = (bf16[128,256]{1,0:T(8,128)(2,1)S(1)}, bf16[128,256]{1,0:T(8,128)(2,1)}, u32[]{:S(2)}) copy-start(bf16[128,256]{1,0:T(8,128)(2,1)} %constant.6.clone.high_far.wide_high) | copy-start | bytes 196612
  33.9 17.8 %copy-start.2 = (f32[16,128]{1,0:T(8,128)S(1)}, f32[16,128]{1,0:T(8,128)}, u32[]{:S(2)}) copy-start(f32[16,128]{1,0:T(8,128)} %constant.8.clone.twiddle_far.twiddle) | copy-start | bytes 24580

commit v3 on v2

--- a/solution.py
+++ b/solution.py
@@ -236,27 +236,33 @@
             left[0] * right[1] + left[1] * right[0],
         )
 
-    mixed = []
+    owns = []
     for place in range(COEF // 4):
-        own = []
         for part in range(2):
             one, two = spectra[2 * place][part], spectra[2 * place + 1][part]
-            own.append(
+            owns.append(
                 jnp.concatenate(
                     [jnp.where(limb_low, one, roll(two, 4)), jnp.where(limb_low, roll(one, -4), two)], axis=0
                 )
             )
-        special = mix(extend, jnp.concatenate(own, axis=1), ((1,), (0,)))
-        own = tensor(own)
-        special = tensor((special[:, :LANES], special[:, LANES:]))
-        products = jnp.concatenate(
-            [jnp.concatenate(own, axis=1), jnp.concatenate(special, axis=1)], axis=0
-        )
-        scaled = mix(shrink, products, ((0,), (0,)))
+    specials = mix(extend, jnp.concatenate(owns, axis=1), ((1,), (0,)))
+    own_products, special_products = [], []
+    for place in range(COEF // 4):
+        start = place * 2 * LANES
+        own_products += tensor(owns[2 * place : 2 * place + 2])
+        special_products += tensor(
+            (specials[:, start : start + LANES], specials[:, start + LANES : start + 2 * LANES])
+        )
+    products = jnp.concatenate(
+        [jnp.concatenate(own_products, axis=1), jnp.concatenate(special_products, axis=1)], axis=0
+    )
+    scaled = mix(shrink, products, ((0,), (0,)))
+    mixed = []
+    for place in range(COEF // 4):
         parts = []
         for part in range(2):
-            both = scaled[:, part * LANES : (part + 1) * LANES]
-            low, high = both[:8], both[8:]
+            start = (2 * place + part) * LANES
+            low, high = scaled[:8, start : start + LANES], scaled[8:, start : start + LANES]
             parts.append((jnp.where(limb_low, low, roll(high, 4)), jnp.where(limb_low, roll(low, -4), high)))
         mixed.append((parts[0][0], parts[1][0]))
         mixed.append((parts[0][1], parts[1][1]))

time: 53 us -> 52.4 us (0.989)
  Pallas kernels: 3.85 us -> 3.28 us
    pallas_call x1, Pallas kernels: 1.54 us -> 0.96 us  [per_device(): pl.pallas_call(tensor_kernel, out_shape=jax.ShapeDtypeStruct((ROOTS, LANE...]
where the time goes in v3:
time: 52.4 us; the launch traced here: 52.1 us
  blocking collectives  48.8 us (93%)
  Pallas kernels  3.28 us (6%)
    all_to_all x1, blocking collectives, per_device(): lax.all_to_all(spectra.reshape(ROOTS, 2, LANES), ('limb', 'coef'), 0, 0)  31 us
    all_to_all x1, blocking collectives, per_device(): lax.all_to_all(scaled.reshape(ROOTS, 1, LANES), ('limb', 'coef'), 0, 0)  17.8 us
    pallas_call x1, Pallas kernels, per_device(): pl.pallas_call(evaluate_kernel, out_shape=jax.ShapeDtypeStruct((2 * ROOTS...  1.34 us

profile of v3, /device:TPU:1, one launch (start us, length us, event | category | flops | bytes accessed | tf_op | source)
XLA Modules:
  0.0 52.1 jit_solution(149943032408950846)
XLA Ops:
  0.0 1.3 %evaluate.1 = f32[512,128]{1,0:T(8,128)S(1)} custom-call(f32[2,2,2,1024]{3,2,1,0:T(2,128)} %first_far.1, f32[2,2,2,1024]{3,2,1,0:T(2,128)} %second_far.1, f32[2,16]{1,0:T(2,128)} %bitcast.13, f32[2,16]{1,0:T(2,128)} %bitcast.14, bf16[128,256]{1,0:T(8,128)(2,1)} %constant.6.clone.high_far.wide_high, bf16[128,256]{1,0:T(8,128)(2,1)} %constant.7.clone.low_far.wide_low, ...), custom_call_target="tpu_custom_call" | custom-call | tf_op jit(solution)/shard_map/evaluate/pallas_call | solution.py:341
  1.3 0.0 copy-start.3
  1.4 31.0 %all_to_all.10 = f32[256,2,128]{2,1,0:T(2,128)S(1)} all-to-all(f32[256,2,128]{2,1,0:T(2,128)S(1)} %bitcast.9), channel_id=1, replica_groups=mesh['limb'=8,'coef'=32] {'limb','coef'}, dimensions={0} | all-to-all | bytes 524288 | tf_op jit(solution)/shard_map/all_to_all | solution.py:360
  32.3 0.0 copy-done.3
  32.3 1.0 %tensor.1 = f32[256,128]{1,0:T(8,128)S(1)} custom-call(f32[512,128]{1,0:T(8,128)S(1)} %bitcast.10, f32[16,16]{1,0:T(8,128)S(1)} %copy-done.3), custom_call_target="tpu_custom_call" | custom-call | tf_op jit(solution)/shard_map/tensor/pallas_call | solution.py:361
  33.3 0.0 copy-start
  33.3 0.0 copy-start.1
  33.3 0.0 copy-start.2
  33.3 17.8 %all_to_all.11 = f32[256,1,128]{2,1,0:T(1,128)S(1)} all-to-all(f32[256,1,128]{2,1,0:T(1,128)S(1)} %bitcast.11), channel_id=1, replica_groups=mesh['limb'=8,'coef'=32] {'limb','coef'}, dimensions={0} | all-to-all | bytes 262144 | tf_op jit(solution)/shard_map/all_to_all | solution.py:369
  51.2 0.0 copy-done
  51.2 0.0 copy-done.1
  51.2 0.0 copy-done.2
  51.2 1.0 %restore.1 = f32[2,3,2,1024]{3,2,1,0:T(2,128)} custom-call(f32[256,128]{1,0:T(8,128)S(1)} %bitcast.12, bf16[128,256]{1,0:T(8,128)(2,1)S(1)} %copy-done.1, bf16[128,256]{1,0:T(8,128)(2,1)S(1)} %copy-done, f32[16,128]{1,0:T(8,128)S(1)} %copy-done.2), custom_call_target="tpu_custom_call" | custom-call | tf_op jit(solution)/shard_map/restore/pallas_call | solution.py:370
Async XLA Ops:
  1.3 31.0 %copy-start.3 = (f32[16,16]{1,0:T(8,128)S(1)}, f32[16,16]{1,0:T(8,128)}, u32[]{:S(2)}) copy-start(f32[16,16]{1,0:T(8,128)} %to_special.1) | copy-start | bytes 3076
  33.3 17.9 %copy-start = (bf16[128,256]{1,0:T(8,128)(2,1)S(1)}, bf16[128,256]{1,0:T(8,128)(2,1)}, u32[]{:S(2)}) copy-start(bf16[128,256]{1,0:T(8,128)(2,1)} %constant.7.clone.low_far.wide_low) | copy-start | bytes 196612
  33.3 17.9 %copy-start.1 = (bf16[128,256]{1,0:T(8,128)(2,1)S(1)}, bf16[128,256]{1,0:T(8,128)(2,1)}, u32[]{:S(2)}) copy-start(bf16[128,256]{1,0:T(8,128)(2,1)} %constant.6.clone.high_far.wide_high) | copy-start | bytes 196612
  33.3 17.8 %copy-start.2 = (f32[16,128]{1,0:T(8,128)S(1)}, f32[16,128]{1,0:T(8,128)}, u32[]{:S(2)}) copy-start(f32[16,128]{1,0:T(8,128)} %constant.8.clone.twiddle_far.twiddle) | copy-start | bytes 24580

commit v4 on v3

--- a/solution.py
+++ b/solution.py
@@ -120,7 +120,13 @@
     rows = jnp.concatenate(blocks, axis=0)
     copies[3].wait()
     copies[4].wait()
-    spectrum = dot3((wide_high[...], wide_low[...]), split_value(rows), ((1,), (1,)))
+    parted = split_value(rows)
+    spectrum = lax.dot_general(
+        jnp.concatenate([wide_high[...], wide_high[...], wide_low[...]], axis=1),
+        jnp.concatenate([parted[0], parted[1], parted[0]], axis=1),
+        (((1,), (1,)), ((), ())),
+        preferred_element_type=f32,
+    )
     copies[5].wait()
     copies[6].wait()
     lane = lax.broadcasted_iota(jnp.int32, (8, LANES), 1)
@@ -138,6 +144,12 @@
 
 def complex_scale(value, cosine, sine):
     real, imag = value
+    if abs(cosine) < 1e-9:
+        return (-imag, real) if sine > 0 else (imag, -real)
+    if abs(abs(cosine) - abs(sine)) < 1e-9:
+        if cosine * sine > 0:
+            return (real - imag) * cosine, (real + imag) * cosine
+        return (real + imag) * cosine, (imag - real) * cosine
     return real * cosine - imag * sine, real * sine + imag * cosine
 
 
@@ -203,27 +215,15 @@
             for part in split_value(rows)
         )
     )
-    table = spread[pl.ds(1, GROUPS, stride=2 * COEF), :]
+    table = spread[pl.ds(1, GROUPS, stride=2), :]
     shrink = split_value(jnp.concatenate([table[:, 16 * j : 16 * j + 16] for j in range(4)], axis=0))
 
-    packed = []
-    for e in range(COEF // 2):
-        even = spread[pl.ds(4 * e, GROUPS, stride=2 * COEF), :]
-        odd = spread[pl.ds(4 * e + 2, GROUPS, stride=2 * COEF), :]
-        packed.append((jnp.where(half, even, roll(odd, 64)), jnp.where(half, roll(even, 64), odd)))
+    blocks = [spread[pl.ds(2 * GROUPS * c, GROUPS, stride=2), :] for c in range(COEF)]
     spectra = []
-    for theta, (real, imag) in split_ring(packed, math.pi):
-        cosine = sign * math.cos(theta / 2)
-        sine = sign * math.sin(theta / 2)
-        real_other, imag_other = roll(real, 64), roll(imag, 64)
-        real_low, imag_low = jnp.where(half, real, real_other), jnp.where(half, imag, imag_other)
-        real_high, imag_high = jnp.where(half, real_other, real), jnp.where(half, imag_other, imag)
-        spectra.append(
-            (
-                real_low + (cosine * real_high - sine * imag_high),
-                imag_low + (cosine * imag_high + sine * real_high),
-            )
-        )
+    for _, (real, imag) in split_ring(list(zip(blocks[: COEF // 2], blocks[COEF // 2 :])), math.pi / 2):
+        one = real - roll(imag, 64)
+        two = imag + roll(real, 64)
+        spectra.append((jnp.where(half, one, two), jnp.where(half, two, one)))
 
     def tensor(value):
         left, right = [], []
@@ -269,24 +269,20 @@
 
     share = 1.0 / (COEF * BLOCK)
     joined = []
-    for (real, imag), theta in zip(mixed, root_angles(COEF // 2, math.pi)):
-        real_other, imag_other = roll(real, 64), roll(imag, 64)
-        root = complex(math.cos(theta / 2), math.sin(theta / 2))
-        plus, minus = (1 - 1j * root) * share, (1 + 1j * root) * share
-        own = (plus, -root.conjugate() * minus)
-        other = (minus, root.conjugate() * plus)
-        own_real, own_imag = jnp.where(half, own[0].real, own[1].real), jnp.where(half, own[0].imag, own[1].imag)
-        other_real = jnp.where(half, other[0].real, other[1].real)
-        other_imag = jnp.where(half, other[0].imag, other[1].imag)
+    for (real, imag), theta in zip(mixed, root_angles(COEF // 2, math.pi / 2)):
+        cosine = share + sign * (share * math.sin(theta))
+        sine = -share * math.cos(theta)
+        own_real, own_imag = real * cosine - imag * sine, imag * cosine + real * sine
+        other_real, other_imag = roll(own_real, 64), roll(own_imag, 64)
         joined.append(
             (
-                (own_real * real - own_imag * imag) + (other_real * real_other - other_imag * imag_other),
-                (own_real * imag + own_imag * real) + (other_real * imag_other + other_imag * real_other),
+                jnp.where(half, own_real + other_real, own_imag + other_imag),
+                jnp.where(half, own_imag - other_imag, own_real - other_real),
             )
         )
-    for e, (real, imag) in enumerate(join_ring(joined, math.pi)):
-        out[pl.ds(2 * e, GROUPS, stride=COEF), :] = jnp.where(half, real, roll(imag, 64))
-        out[pl.ds(2 * e + 1, GROUPS, stride=COEF), :] = jnp.where(half, roll(real, 64), imag)
+    for c, (real, imag) in enumerate(join_ring(joined, math.pi / 2)):
+        out[GROUPS * c : GROUPS * (c + 1), :] = real
+        out[GROUPS * (c + COEF // 2) : GROUPS * (c + COEF // 2 + 1), :] = imag
 
 
 def restore_kernel(gathered, wide_high, wide_low, twiddle, out):
@@ -357,7 +353,7 @@
         compiler_params=params,
         name="evaluate",
     )(*kept_far(first_cipher, second_cipher, keep_table.T, scale_table.T, wide_high, wide_low, twiddle))
-    spread = lax.all_to_all(spectra.reshape(ROOTS, 2, LANES), ("limb", "coef"), 0, 0)
+    spread = lax.all_to_all(spectra.reshape(ROOTS, 2, LANES), ("coef", "limb"), 0, 0)
     scaled = pl.pallas_call(
         tensor_kernel,
         out_shape=jax.ShapeDtypeStruct((ROOTS, LANES), f32),
@@ -366,7 +362,7 @@
         compiler_params=params,
         name="tensor",
     )(spread.reshape(2 * ROOTS, LANES), to_special)
-    gathered = lax.all_to_all(scaled.reshape(ROOTS, 1, LANES), ("limb", "coef"), 0, 0)
+    gathered = lax.all_to_all(scaled.reshape(ROOTS, 1, LANES), ("coef", "limb"), 0, 0)
     product = pl.pallas_call(
         restore_kernel,
         out_shape=jax.ShapeDtypeStruct((2, 3, 2, BLOCK), f32),

time: 52.4 us -> 52.9 us (level)
  blocking collectives: 48.8 us -> 49.5 us
    all_to_all x2, blocking collectives: 48.8 us -> 49.5 us  [the longest x1 31.3 us: per_device(): lax.all_to_all(spectra.reshape(ROOTS, 2, LANES), ('coef', 'limb'), 0, 0)]
where the time goes in v4:
time: 52.9 us; the launch traced here: 52.6 us
  blocking collectives  49.5 us (94%)
  Pallas kernels  3.06 us (6%)
    all_to_all x1, blocking collectives, per_device(): lax.all_to_all(spectra.reshape(ROOTS, 2, LANES), ('coef', 'limb'), 0, 0)  31.3 us
    all_to_all x1, blocking collectives, per_device(): lax.all_to_all(scaled.reshape(ROOTS, 1, LANES), ('coef', 'limb'), 0, 0)  18.2 us
    pallas_call x1, Pallas kernels, per_device(): pl.pallas_call(evaluate_kernel, out_shape=jax.ShapeDtypeStruct((2 * ROOTS...  1.34 us

profile of v4, /device:TPU:1, one launch (start us, length us, event | category | flops | bytes accessed | tf_op | source)
XLA Modules:
  0.0 52.6 jit_solution(17431621668911964306)
XLA Ops:
  0.0 1.3 %evaluate.1 = f32[512,128]{1,0:T(8,128)S(1)} custom-call(f32[2,2,2,1024]{3,2,1,0:T(2,128)} %first_far.1, f32[2,2,2,1024]{3,2,1,0:T(2,128)} %second_far.1, f32[2,16]{1,0:T(2,128)} %bitcast.13, f32[2,16]{1,0:T(2,128)} %bitcast.14, bf16[128,256]{1,0:T(8,128)(2,1)} %constant.6.clone.high_far.wide_high, bf16[128,256]{1,0:T(8,128)(2,1)} %constant.7.clone.low_far.wide_low, ...), custom_call_target="tpu_custom_call" | custom-call | tf_op jit(solution)/shard_map/evaluate/pallas_call | solution.py:337
  1.3 0.0 copy-start.3
  1.4 31.3 %all_to_all.10 = f32[256,2,128]{2,1,0:T(2,128)S(1)} all-to-all(f32[256,2,128]{2,1,0:T(2,128)S(1)} %bitcast.9), channel_id=1, replica_groups=mesh['limb'=8,'coef'=32] {'coef','limb'}, dimensions={0} | all-to-all | bytes 524288 | tf_op jit(solution)/shard_map/all_to_all | solution.py:356
  32.6 0.0 copy-done.3
  32.6 0.8 %tensor.1 = f32[256,128]{1,0:T(8,128)S(1)} custom-call(f32[512,128]{1,0:T(8,128)S(1)} %bitcast.10, f32[16,16]{1,0:T(8,128)S(1)} %copy-done.3), custom_call_target="tpu_custom_call" | custom-call | tf_op jit(solution)/shard_map/tensor/pallas_call | solution.py:357
  33.4 0.0 copy-start
  33.4 0.0 copy-start.1
  33.4 0.0 copy-start.2
  33.4 18.2 %all_to_all.11 = f32[256,1,128]{2,1,0:T(1,128)S(1)} all-to-all(f32[256,1,128]{2,1,0:T(1,128)S(1)} %bitcast.11), channel_id=1, replica_groups=mesh['limb'=8,'coef'=32] {'coef','limb'}, dimensions={0} | all-to-all | bytes 262144 | tf_op jit(solution)/shard_map/all_to_all | solution.py:365
  51.6 0.0 copy-done
  51.6 0.0 copy-done.1
  51.6 0.0 copy-done.2
  51.7 1.0 %restore.1 = f32[2,3,2,1024]{3,2,1,0:T(2,128)} custom-call(f32[256,128]{1,0:T(8,128)S(1)} %bitcast.12, bf16[128,256]{1,0:T(8,128)(2,1)S(1)} %copy-done.1, bf16[128,256]{1,0:T(8,128)(2,1)S(1)} %copy-done, f32[16,128]{1,0:T(8,128)S(1)} %copy-done.2), custom_call_target="tpu_custom_call" | custom-call | tf_op jit(solution)/shard_map/restore/pallas_call | solution.py:366
Async XLA Ops:
  1.3 31.3 %copy-start.3 = (f32[16,16]{1,0:T(8,128)S(1)}, f32[16,16]{1,0:T(8,128)}, u32[]{:S(2)}) copy-start(f32[16,16]{1,0:T(8,128)} %to_special.1) | copy-start | bytes 3076
  33.4 18.3 %copy-start = (bf16[128,256]{1,0:T(8,128)(2,1)S(1)}, bf16[128,256]{1,0:T(8,128)(2,1)}, u32[]{:S(2)}) copy-start(bf16[128,256]{1,0:T(8,128)(2,1)} %constant.7.clone.low_far.wide_low) | copy-start | bytes 196612
  33.4 18.2 %copy-start.1 = (bf16[128,256]{1,0:T(8,128)(2,1)S(1)}, bf16[128,256]{1,0:T(8,128)(2,1)}, u32[]{:S(2)}) copy-start(bf16[128,256]{1,0:T(8,128)(2,1)} %constant.6.clone.high_far.wide_high) | copy-start | bytes 196612
  33.4 18.2 %copy-start.2 = (f32[16,128]{1,0:T(8,128)S(1)}, f32[16,128]{1,0:T(8,128)}, u32[]{:S(2)}) copy-start(f32[16,128]{1,0:T(8,128)} %constant.8.clone.twiddle_far.twiddle) | copy-start | bytes 24580

commit v5 on v4

--- a/solution.py
+++ b/solution.py
@@ -215,10 +215,10 @@
             for part in split_value(rows)
         )
     )
-    table = spread[pl.ds(1, GROUPS, stride=2), :]
+    table = spread[pl.ds(1, GROUPS, stride=2 * COEF), :]
     shrink = split_value(jnp.concatenate([table[:, 16 * j : 16 * j + 16] for j in range(4)], axis=0))
 
-    blocks = [spread[pl.ds(2 * GROUPS * c, GROUPS, stride=2), :] for c in range(COEF)]
+    blocks = [spread[pl.ds(2 * c, GROUPS, stride=2 * COEF), :] for c in range(COEF)]
     spectra = []
     for _, (real, imag) in split_ring(list(zip(blocks[: COEF // 2], blocks[COEF // 2 :])), math.pi / 2):
         one = real - roll(imag, 64)
@@ -281,17 +281,19 @@
             )
         )
     for c, (real, imag) in enumerate(join_ring(joined, math.pi / 2)):
-        out[GROUPS * c : GROUPS * (c + 1), :] = real
-        out[GROUPS * (c + COEF // 2) : GROUPS * (c + COEF // 2 + 1), :] = imag
+        out[pl.ds(c, GROUPS, stride=COEF), :] = real
+        out[pl.ds(c + COEF // 2, GROUPS, stride=COEF), :] = imag
 
 
 def restore_kernel(gathered, wide_high, wide_low, twiddle, out):
     row = lax.broadcasted_iota(jnp.int32, (8, LANES), 0)
     middle = (row & 3) == 1
-    wide = (wide_high[...], wide_low[...])
+    values = split_value(jnp.concatenate([gathered[:LANES, :], gathered[LANES:, :]], axis=1))
+    left = jnp.concatenate([values[0], values[1], values[0]], axis=0)
+    right = jnp.concatenate([wide_high[...], wide_high[...], wide_low[...]], axis=0)
+    both = lax.dot_general(left, right, (((0,), (0,)), ((), ())), preferred_element_type=f32)
     for pair in range(2):
-        values = gathered[pair * LANES : (pair + 1) * LANES, :]
-        spun = dot3(split_value(values), wide, ((0,), (0,)))
+        spun = both[pair * LANES : (pair + 1) * LANES]
         real = spun[:64, :LANES] + spun[64:, LANES:]
         imag = spun[64:, :LANES] - spun[:64, LANES:]
         turned = []
@@ -353,7 +355,7 @@
         compiler_params=params,
         name="evaluate",
     )(*kept_far(first_cipher, second_cipher, keep_table.T, scale_table.T, wide_high, wide_low, twiddle))
-    spread = lax.all_to_all(spectra.reshape(ROOTS, 2, LANES), ("coef", "limb"), 0, 0)
+    spread = lax.all_to_all(spectra.reshape(ROOTS, 2, LANES), ("limb", "coef"), 0, 0)
     scaled = pl.pallas_call(
         tensor_kernel,
         out_shape=jax.ShapeDtypeStruct((ROOTS, LANES), f32),
@@ -362,7 +364,7 @@
         compiler_params=params,
         name="tensor",
     )(spread.reshape(2 * ROOTS, LANES), to_special)
-    gathered = lax.all_to_all(scaled.reshape(ROOTS, 1, LANES), ("coef", "limb"), 0, 0)
+    gathered = lax.all_to_all(scaled.reshape(ROOTS, 1, LANES), ("limb", "coef"), 0, 0)
     product = pl.pallas_call(
         restore_kernel,
         out_shape=jax.ShapeDtypeStruct((2, 3, 2, BLOCK), f32),

time: 52.9 us -> 52.2 us (0.987)
  blocking collectives: 49.5 us -> 48.8 us
    all_to_all x2, blocking collectives: 49.5 us -> 48.8 us  [the longest x1 31 us: per_device(): lax.all_to_all(spectra.reshape(ROOTS, 2, LANES), ('limb', 'coef'), 0, 0)]
where the time goes in v5:
time: 52.2 us; the launch traced here: 52 us
  blocking collectives  48.8 us (93%)
  Pallas kernels  3.14 us (6%)
    all_to_all x1, blocking collectives, per_device(): lax.all_to_all(spectra.reshape(ROOTS, 2, LANES), ('limb', 'coef'), 0, 0)  31 us
    all_to_all x1, blocking collectives, per_device(): lax.all_to_all(scaled.reshape(ROOTS, 1, LANES), ('limb', 'coef'), 0, 0)  17.8 us
    pallas_call x1, Pallas kernels, per_device(): pl.pallas_call(evaluate_kernel, out_shape=jax.ShapeDtypeStruct((2 * ROOTS...  1.34 us

profile of v5, /device:TPU:1, one launch (start us, length us, event | category | flops | bytes accessed | tf_op | source)
XLA Modules:
  0.0 52.0 jit_solution(6823559195294348128)
XLA Ops:
  0.0 1.3 %evaluate.1 = f32[512,128]{1,0:T(8,128)S(1)} custom-call(f32[2,2,2,1024]{3,2,1,0:T(2,128)} %first_far.1, f32[2,2,2,1024]{3,2,1,0:T(2,128)} %second_far.1, f32[2,16]{1,0:T(2,128)} %bitcast.13, f32[2,16]{1,0:T(2,128)} %bitcast.14, bf16[128,256]{1,0:T(8,128)(2,1)} %constant.6.clone.high_far.wide_high, bf16[128,256]{1,0:T(8,128)(2,1)} %constant.7.clone.low_far.wide_low, ...), custom_call_target="tpu_custom_call" | custom-call | tf_op jit(solution)/shard_map/evaluate/pallas_call | solution.py:339
  1.3 0.0 copy-start.3
  1.4 31.0 %all_to_all.10 = f32[256,2,128]{2,1,0:T(2,128)S(1)} all-to-all(f32[256,2,128]{2,1,0:T(2,128)S(1)} %bitcast.9), channel_id=1, replica_groups=mesh['limb'=8,'coef'=32] {'limb','coef'}, dimensions={0} | all-to-all | bytes 524288 | tf_op jit(solution)/shard_map/all_to_all | solution.py:358
  32.3 0.0 copy-done.3
  32.3 0.9 %tensor.1 = f32[256,128]{1,0:T(8,128)S(1)} custom-call(f32[512,128]{1,0:T(8,128)S(1)} %bitcast.10, f32[16,16]{1,0:T(8,128)S(1)} %copy-done.3), custom_call_target="tpu_custom_call" | custom-call | tf_op jit(solution)/shard_map/tensor/pallas_call | solution.py:359
  33.2 0.0 copy-start
  33.2 0.0 copy-start.1
  33.2 0.0 copy-start.2
  33.3 17.8 %all_to_all.11 = f32[256,1,128]{2,1,0:T(1,128)S(1)} all-to-all(f32[256,1,128]{2,1,0:T(1,128)S(1)} %bitcast.11), channel_id=1, replica_groups=mesh['limb'=8,'coef'=32] {'limb','coef'}, dimensions={0} | all-to-all | bytes 262144 | tf_op jit(solution)/shard_map/all_to_all | solution.py:367
  51.1 0.0 copy-done
  51.1 0.0 copy-done.1
  51.1 0.0 copy-done.2
  51.1 0.9 %restore.1 = f32[2,3,2,1024]{3,2,1,0:T(2,128)} custom-call(f32[256,128]{1,0:T(8,128)S(1)} %bitcast.12, bf16[128,256]{1,0:T(8,128)(2,1)S(1)} %copy-done.1, bf16[128,256]{1,0:T(8,128)(2,1)S(1)} %copy-done, f32[16,128]{1,0:T(8,128)S(1)} %copy-done.2), custom_call_target="tpu_custom_call" | custom-call | tf_op jit(solution)/shard_map/restore/pallas_call | solution.py:368
Async XLA Ops:
  1.3 31.0 %copy-start.3 = (f32[16,16]{1,0:T(8,128)S(1)}, f32[16,16]{1,0:T(8,128)}, u32[]{:S(2)}) copy-start(f32[16,16]{1,0:T(8,128)} %to_special.1) | copy-start | bytes 3076
  33.2 17.9 %copy-start = (bf16[128,256]{1,0:T(8,128)(2,1)S(1)}, bf16[128,256]{1,0:T(8,128)(2,1)}, u32[]{:S(2)}) copy-start(bf16[128,256]{1,0:T(8,128)(2,1)} %constant.7.clone.low_far.wide_low) | copy-start | bytes 196612
  33.2 17.9 %copy-start.1 = (bf16[128,256]{1,0:T(8,128)(2,1)S(1)}, bf16[128,256]{1,0:T(8,128)(2,1)}, u32[]{:S(2)}) copy-start(bf16[128,256]{1,0:T(8,128)(2,1)} %constant.6.clone.high_far.wide_high) | copy-start | bytes 196612
  33.2 17.8 %copy-start.2 = (f32[16,128]{1,0:T(8,128)S(1)}, f32[16,128]{1,0:T(8,128)}, u32[]{:S(2)}) copy-start(f32[16,128]{1,0:T(8,128)} %constant.8.clone.twiddle_far.twiddle) | copy-start | bytes 24580

commit v6 on v5

--- a/solution.py
+++ b/solution.py
@@ -87,6 +87,17 @@
                         limb, pair, :, u * LANES : (u + 1) * LANES
                     ]
     copies[2].wait()
+    copies[5].wait()
+    copies[6].wait()
+    lane = lax.broadcasted_iota(jnp.int32, (8, LANES), 1)
+    table = jnp.zeros((8, LANES), f32)
+    for i in range(16):
+        for limb in range(2):
+            place = limb * 16 + (i % 2) * 8 + i // 2
+            table = jnp.where(lane == place, keep[limb, i], table)
+            table = jnp.where(lane == 32 + place, scale[limb, i], table)
+    for tile in range(ROOTS // 8):
+        out[pl.ds(tile * 16 + 1, 8, stride=2), :] = table
     blocks = []
     for pair in range(2):
         parts = [held[(pair * U + u) * 8 : (pair * U + u + 1) * 8, :] for u in range(U)]
@@ -127,19 +138,8 @@
         (((1,), (1,)), ((), ())),
         preferred_element_type=f32,
     )
-    copies[5].wait()
-    copies[6].wait()
-    lane = lax.broadcasted_iota(jnp.int32, (8, LANES), 1)
-    table = jnp.zeros((8, LANES), f32)
-    for i in range(16):
-        for limb in range(2):
-            place = limb * 16 + (i % 2) * 8 + i // 2
-            table = jnp.where(lane == place, keep[limb, i], table)
-            table = jnp.where(lane == 32 + place, scale[limb, i], table)
     for pair in range(2):
         out[pl.ds(pair * 256, LANES, stride=2), :] = spectrum[:, pair * LANES : (pair + 1) * LANES]
-    for tile in range(ROOTS // 8):
-        out[pl.ds(tile * 16 + 1, 8, stride=2), :] = table
 
 
 def complex_scale(value, cosine, sine):
@@ -349,7 +349,7 @@
             pltpu.VMEM(wide_high.shape, bf16),
             pltpu.VMEM(wide_low.shape, bf16),
             pltpu.VMEM(twiddle.shape, f32),
-            pltpu.VMEM((2 * U * 8, LANES), f32),
+            pltpu.VMEM((2 * U * 8 + 16, LANES), f32),
             pltpu.SemaphoreType.DMA((7,)),
         ],
         compiler_params=params,

time: 52.2 us -> 52.2 us (level)
  no operation moved by 1% of the time
where the time goes in v6:
time: 52.2 us; the launch traced here: 52 us
  blocking collectives  48.8 us (93%)
  Pallas kernels  3.08 us (6%)
    all_to_all x1, blocking collectives, per_device(): lax.all_to_all(spectra.reshape(ROOTS, 2, LANES), ('limb', 'coef'), 0, 0)  31 us
    all_to_all x1, blocking collectives, per_device(): lax.all_to_all(scaled.reshape(ROOTS, 1, LANES), ('limb', 'coef'), 0, 0)  17.8 us
    pallas_call x1, Pallas kernels, per_device(): pl.pallas_call(evaluate_kernel, out_shape=jax.ShapeDtypeStruct((2 * ROOTS...  1.27 us

profile of v6, /device:TPU:1, one launch (start us, length us, event | category | flops | bytes accessed | tf_op | source)
XLA Modules:
  0.0 52.0 jit_solution(1708003560586773596)
XLA Ops:
  0.0 1.3 %evaluate.1 = f32[512,128]{1,0:T(8,128)S(1)} custom-call(f32[2,2,2,1024]{3,2,1,0:T(2,128)} %first_far.1, f32[2,2,2,1024]{3,2,1,0:T(2,128)} %second_far.1, f32[2,16]{1,0:T(2,128)} %bitcast.13, f32[2,16]{1,0:T(2,128)} %bitcast.14, bf16[128,256]{1,0:T(8,128)(2,1)} %constant.6.clone.high_far.wide_high, bf16[128,256]{1,0:T(8,128)(2,1)} %constant.7.clone.low_far.wide_low, ...), custom_call_target="tpu_custom_call" | custom-call | tf_op jit(solution)/shard_map/evaluate/pallas_call | solution.py:339
  1.3 0.0 copy-start.3
  1.3 31.0 %all_to_all.10 = f32[256,2,128]{2,1,0:T(2,128)S(1)} all-to-all(f32[256,2,128]{2,1,0:T(2,128)S(1)} %bitcast.9), channel_id=1, replica_groups=mesh['limb'=8,'coef'=32] {'limb','coef'}, dimensions={0} | all-to-all | bytes 524288 | tf_op jit(solution)/shard_map/all_to_all | solution.py:358
  32.3 0.0 copy-done.3
  32.3 0.9 %tensor.1 = f32[256,128]{1,0:T(8,128)S(1)} custom-call(f32[512,128]{1,0:T(8,128)S(1)} %bitcast.10, f32[16,16]{1,0:T(8,128)S(1)} %copy-done.3), custom_call_target="tpu_custom_call" | custom-call | tf_op jit(solution)/shard_map/tensor/pallas_call | solution.py:359
  33.2 0.0 copy-start
  33.2 0.0 copy-start.1
  33.2 0.0 copy-start.2
  33.2 17.8 %all_to_all.11 = f32[256,1,128]{2,1,0:T(1,128)S(1)} all-to-all(f32[256,1,128]{2,1,0:T(1,128)S(1)} %bitcast.11), channel_id=1, replica_groups=mesh['limb'=8,'coef'=32] {'limb','coef'}, dimensions={0} | all-to-all | bytes 262144 | tf_op jit(solution)/shard_map/all_to_all | solution.py:367
  51.0 0.0 copy-done
  51.0 0.0 copy-done.1
  51.0 0.0 copy-done.2
  51.0 0.9 %restore.1 = f32[2,3,2,1024]{3,2,1,0:T(2,128)} custom-call(f32[256,128]{1,0:T(8,128)S(1)} %bitcast.12, bf16[128,256]{1,0:T(8,128)(2,1)S(1)} %copy-done.1, bf16[128,256]{1,0:T(8,128)(2,1)S(1)} %copy-done, f32[16,128]{1,0:T(8,128)S(1)} %copy-done.2), custom_call_target="tpu_custom_call" | custom-call | tf_op jit(solution)/shard_map/restore/pallas_call | solution.py:368
Async XLA Ops:
  1.3 31.0 %copy-start.3 = (f32[16,16]{1,0:T(8,128)S(1)}, f32[16,16]{1,0:T(8,128)}, u32[]{:S(2)}) copy-start(f32[16,16]{1,0:T(8,128)} %to_special.1) | copy-start | bytes 3076
  33.2 17.9 %copy-start = (bf16[128,256]{1,0:T(8,128)(2,1)S(1)}, bf16[128,256]{1,0:T(8,128)(2,1)}, u32[]{:S(2)}) copy-start(bf16[128,256]{1,0:T(8,128)(2,1)} %constant.7.clone.low_far.wide_low) | copy-start | bytes 196612
  33.2 17.9 %copy-start.1 = (bf16[128,256]{1,0:T(8,128)(2,1)S(1)}, bf16[128,256]{1,0:T(8,128)(2,1)}, u32[]{:S(2)}) copy-start(bf16[128,256]{1,0:T(8,128)(2,1)} %constant.6.clone.high_far.wide_high) | copy-start | bytes 196612
  33.2 17.8 %copy-start.2 = (f32[16,128]{1,0:T(8,128)S(1)}, f32[16,128]{1,0:T(8,128)}, u32[]{:S(2)}) copy-start(f32[16,128]{1,0:T(8,128)} %constant.8.clone.twiddle_far.twiddle) | copy-start | bytes 24580

commit v7 on v6

--- a/solution.py
+++ b/solution.py
@@ -131,13 +131,16 @@
     rows = jnp.concatenate(blocks, axis=0)
     copies[3].wait()
     copies[4].wait()
-    parted = split_value(rows)
-    spectrum = lax.dot_general(
-        jnp.concatenate([wide_high[...], wide_high[...], wide_low[...]], axis=1),
-        jnp.concatenate([parted[0], parted[1], parted[0]], axis=1),
-        (((1,), (1,)), ((), ())),
-        preferred_element_type=f32,
-    )
+    left = jnp.concatenate([wide_high[...], wide_high[...], wide_low[...]], axis=1)
+    halves = []
+    for pair in range(2):
+        high, low = split_value(jnp.concatenate(blocks[2 * pair : 2 * pair + 2], axis=0))
+        halves.append(
+            lax.dot_general(
+                left, jnp.concatenate([high, low, high], axis=1), (((1,), (1,)), ((), ())), preferred_element_type=f32
+            )
+        )
+    spectrum = jnp.concatenate(halves, axis=1)
     for pair in range(2):
         out[pl.ds(pair * 256, LANES, stride=2), :] = spectrum[:, pair * LANES : (pair + 1) * LANES]
 
@@ -226,15 +229,9 @@
         spectra.append((jnp.where(half, one, two), jnp.where(half, two, one)))
 
     def tensor(value):
-        left, right = [], []
-        for part in value:
-            after = roll(part, -1)
-            left.append(jnp.where(comp == 1, after, jnp.where(comp == 3, roll(part, 3), part)))
-            right.append(jnp.where((comp & 1) == 0, after, part))
-        return (
-            left[0] * right[0] - left[1] * right[1],
-            left[0] * right[1] + left[1] * right[0],
-        )
+        real, imag = value
+        real_next, imag_next = (jnp.where(comp == 3, roll(part, 3), roll(part, -1)) for part in value)
+        return real * real_next - imag * imag_next, real * imag_next + imag * real_next
 
     owns = []
     for place in range(COEF // 4):

time: 52.2 us -> 52.2 us (level)
  no operation moved by 1% of the time
where the time goes in v7:
time: 52.2 us; the launch traced here: 51.9 us
  blocking collectives  48.8 us (93%)
  Pallas kernels  3.06 us (6%)
    all_to_all x1, blocking collectives, per_device(): lax.all_to_all(spectra.reshape(ROOTS, 2, LANES), ('limb', 'coef'), 0, 0)  31 us
    all_to_all x1, blocking collectives, per_device(): lax.all_to_all(scaled.reshape(ROOTS, 1, LANES), ('limb', 'coef'), 0, 0)  17.8 us
    pallas_call x1, Pallas kernels, per_device(): pl.pallas_call(evaluate_kernel, out_shape=jax.ShapeDtypeStruct((2 * ROOTS...  1.25 us

profile of v7, /device:TPU:1, one launch (start us, length us, event | category | flops | bytes accessed | tf_op | source)
XLA Modules:
  0.0 51.9 jit_solution(14160796205162963922)
XLA Ops:
  0.0 1.3 %evaluate.1 = f32[512,128]{1,0:T(8,128)S(1)} custom-call(f32[2,2,2,1024]{3,2,1,0:T(2,128)} %first_far.1, f32[2,2,2,1024]{3,2,1,0:T(2,128)} %second_far.1, f32[2,16]{1,0:T(2,128)} %bitcast.13, f32[2,16]{1,0:T(2,128)} %bitcast.14, bf16[128,256]{1,0:T(8,128)(2,1)} %constant.6.clone.high_far.wide_high, bf16[128,256]{1,0:T(8,128)(2,1)} %constant.7.clone.low_far.wide_low, ...), custom_call_target="tpu_custom_call" | custom-call | tf_op jit(solution)/shard_map/evaluate/pallas_call | solution.py:336
  1.3 0.0 copy-start.3
  1.3 31.0 %all_to_all.10 = f32[256,2,128]{2,1,0:T(2,128)S(1)} all-to-all(f32[256,2,128]{2,1,0:T(2,128)S(1)} %bitcast.9), channel_id=1, replica_groups=mesh['limb'=8,'coef'=32] {'limb','coef'}, dimensions={0} | all-to-all | bytes 524288 | tf_op jit(solution)/shard_map/all_to_all | solution.py:355
  32.2 0.0 copy-done.3
  32.2 0.9 %tensor.1 = f32[256,128]{1,0:T(8,128)S(1)} custom-call(f32[512,128]{1,0:T(8,128)S(1)} %bitcast.10, f32[16,16]{1,0:T(8,128)S(1)} %copy-done.3), custom_call_target="tpu_custom_call" | custom-call | tf_op jit(solution)/shard_map/tensor/pallas_call | solution.py:356
  33.1 0.0 copy-start
  33.1 0.0 copy-start.1
  33.2 0.0 copy-start.2
  33.2 17.8 %all_to_all.11 = f32[256,1,128]{2,1,0:T(1,128)S(1)} all-to-all(f32[256,1,128]{2,1,0:T(1,128)S(1)} %bitcast.11), channel_id=1, replica_groups=mesh['limb'=8,'coef'=32] {'limb','coef'}, dimensions={0} | all-to-all | bytes 262144 | tf_op jit(solution)/shard_map/all_to_all | solution.py:364
  51.0 0.0 copy-done
  51.0 0.0 copy-done.1
  51.0 0.0 copy-done.2
  51.0 0.9 %restore.1 = f32[2,3,2,1024]{3,2,1,0:T(2,128)} custom-call(f32[256,128]{1,0:T(8,128)S(1)} %bitcast.12, bf16[128,256]{1,0:T(8,128)(2,1)S(1)} %copy-done.1, bf16[128,256]{1,0:T(8,128)(2,1)S(1)} %copy-done, f32[16,128]{1,0:T(8,128)S(1)} %copy-done.2), custom_call_target="tpu_custom_call" | custom-call | tf_op jit(solution)/shard_map/restore/pallas_call | solution.py:365
Async XLA Ops:
  1.3 31.0 %copy-start.3 = (f32[16,16]{1,0:T(8,128)S(1)}, f32[16,16]{1,0:T(8,128)}, u32[]{:S(2)}) copy-start(f32[16,16]{1,0:T(8,128)} %to_special.1) | copy-start | bytes 3076
  33.1 17.9 %copy-start = (bf16[128,256]{1,0:T(8,128)(2,1)S(1)}, bf16[128,256]{1,0:T(8,128)(2,1)}, u32[]{:S(2)}) copy-start(bf16[128,256]{1,0:T(8,128)(2,1)} %constant.7.clone.low_far.wide_low) | copy-start | bytes 196612
  33.1 17.9 %copy-start.1 = (bf16[128,256]{1,0:T(8,128)(2,1)S(1)}, bf16[128,256]{1,0:T(8,128)(2,1)}, u32[]{:S(2)}) copy-start(bf16[128,256]{1,0:T(8,128)(2,1)} %constant.6.clone.high_far.wide_high) | copy-start | bytes 196612
  33.2 17.8 %copy-start.2 = (f32[16,128]{1,0:T(8,128)S(1)}, f32[16,128]{1,0:T(8,128)}, u32[]{:S(2)}) copy-start(f32[16,128]{1,0:T(8,128)} %constant.8.clone.twiddle_far.twiddle) | copy-start | bytes 24580

commit v8 on v7

--- a/solution.py
+++ b/solution.py
@@ -303,11 +303,22 @@
         for k0 in range(K0 // 2):
             one, two = turned[k0], turned[k0 + K0 // 2]
             halves.append(((one[0] + two[0], one[1] + two[1]), (one[0] - two[0], one[1] - two[1])))
+        quarters = []
+        for k0 in range(K0 // 4):
+            (even, odd), (even_far, odd_far) = halves[k0], halves[k0 + 2]
+            quarters.append(
+                (
+                    (even[0] + even_far[0], even[1] + even_far[1]),
+                    (odd[0] + odd_far[1], odd[1] - odd_far[0]),
+                    (even[0] - even_far[0], even[1] - even_far[1]),
+                    (odd[0] - odd_far[1], odd[1] + odd_far[0]),
+                )
+            )
         for u in range(U):
             total = None
-            for k0 in range(K0 // 2):
+            for k0 in range(K0 // 4):
                 cosine, sine = turn(u, k0)
-                real_part, imag_part = halves[k0][u % 2]
+                real_part, imag_part = quarters[k0][u % 4]
                 term = real_part if u == 0 else real_part * cosine + imag_part * sine
                 total = term if total is None else total + term
             total = jnp.where(middle, total + pltpu.roll(total, 6, 0), total)

time: 52.2 us -> 52.1 us (level)
  no operation moved by 1% of the time
where the time goes in v8:
time: 52.1 us; the launch traced here: 51.9 us
  blocking collectives  48.8 us (94%)
  Pallas kernels  3.05 us (6%)
    all_to_all x1, blocking collectives, per_device(): lax.all_to_all(spectra.reshape(ROOTS, 2, LANES), ('limb', 'coef'), 0, 0)  31 us
    all_to_all x1, blocking collectives, per_device(): lax.all_to_all(scaled.reshape(ROOTS, 1, LANES), ('limb', 'coef'), 0, 0)  17.8 us
    pallas_call x1, Pallas kernels, per_device(): pl.pallas_call(evaluate_kernel, out_shape=jax.ShapeDtypeStruct((2 * ROOTS...  1.25 us

profile of v8, /device:TPU:1, one launch (start us, length us, event | category | flops | bytes accessed | tf_op | source)
XLA Modules:
  0.0 51.9 jit_solution(14722956641037958417)
XLA Ops:
  0.0 1.3 %evaluate.1 = f32[512,128]{1,0:T(8,128)S(1)} custom-call(f32[2,2,2,1024]{3,2,1,0:T(2,128)} %first_far.1, f32[2,2,2,1024]{3,2,1,0:T(2,128)} %second_far.1, f32[2,16]{1,0:T(2,128)} %bitcast.13, f32[2,16]{1,0:T(2,128)} %bitcast.14, bf16[128,256]{1,0:T(8,128)(2,1)} %constant.6.clone.high_far.wide_high, bf16[128,256]{1,0:T(8,128)(2,1)} %constant.7.clone.low_far.wide_low, ...), custom_call_target="tpu_custom_call" | custom-call | tf_op jit(solution)/shard_map/evaluate/pallas_call | solution.py:347
  1.3 0.0 copy-start.3
  1.3 31.0 %all_to_all.10 = f32[256,2,128]{2,1,0:T(2,128)S(1)} all-to-all(f32[256,2,128]{2,1,0:T(2,128)S(1)} %bitcast.9), channel_id=1, replica_groups=mesh['limb'=8,'coef'=32] {'limb','coef'}, dimensions={0} | all-to-all | bytes 524288 | tf_op jit(solution)/shard_map/all_to_all | solution.py:366
  32.2 0.0 copy-done.3
  32.2 0.9 %tensor.1 = f32[256,128]{1,0:T(8,128)S(1)} custom-call(f32[512,128]{1,0:T(8,128)S(1)} %bitcast.10, f32[16,16]{1,0:T(8,128)S(1)} %copy-done.3), custom_call_target="tpu_custom_call" | custom-call | tf_op jit(solution)/shard_map/tensor/pallas_call | solution.py:367
  33.1 0.0 copy-start
  33.1 0.0 copy-start.1
  33.2 0.0 copy-start.2
  33.2 17.8 %all_to_all.11 = f32[256,1,128]{2,1,0:T(1,128)S(1)} all-to-all(f32[256,1,128]{2,1,0:T(1,128)S(1)} %bitcast.11), channel_id=1, replica_groups=mesh['limb'=8,'coef'=32] {'limb','coef'}, dimensions={0} | all-to-all | bytes 262144 | tf_op jit(solution)/shard_map/all_to_all | solution.py:375
  51.0 0.0 copy-done
  51.0 0.0 copy-done.1
  51.0 0.0 copy-done.2
  51.0 0.9 %restore.1 = f32[2,3,2,1024]{3,2,1,0:T(2,128)} custom-call(f32[256,128]{1,0:T(8,128)S(1)} %bitcast.12, bf16[128,256]{1,0:T(8,128)(2,1)S(1)} %copy-done.1, bf16[128,256]{1,0:T(8,128)(2,1)S(1)} %copy-done, f32[16,128]{1,0:T(8,128)S(1)} %copy-done.2), custom_call_target="tpu_custom_call" | custom-call | tf_op jit(solution)/shard_map/restore/pallas_call | solution.py:376
Async XLA Ops:
  1.3 31.0 %copy-start.3 = (f32[16,16]{1,0:T(8,128)S(1)}, f32[16,16]{1,0:T(8,128)}, u32[]{:S(2)}) copy-start(f32[16,16]{1,0:T(8,128)} %to_special.1) | copy-start | bytes 3076
  33.1 17.9 %copy-start = (bf16[128,256]{1,0:T(8,128)(2,1)S(1)}, bf16[128,256]{1,0:T(8,128)(2,1)}, u32[]{:S(2)}) copy-start(bf16[128,256]{1,0:T(8,128)(2,1)} %constant.7.clone.low_far.wide_low) | copy-start | bytes 196612
  33.1 17.9 %copy-start.1 = (bf16[128,256]{1,0:T(8,128)(2,1)S(1)}, bf16[128,256]{1,0:T(8,128)(2,1)}, u32[]{:S(2)}) copy-start(bf16[128,256]{1,0:T(8,128)(2,1)} %constant.6.clone.high_far.wide_high) | copy-start | bytes 196612
  33.2 17.8 %copy-start.2 = (f32[16,128]{1,0:T(8,128)S(1)}, f32[16,128]{1,0:T(8,128)}, u32[]{:S(2)}) copy-start(f32[16,128]{1,0:T(8,128)} %constant.8.clone.twiddle_far.twiddle) | copy-start | bytes 24580

commit v9 on v8

--- a/solution.py
+++ b/solution.py
@@ -102,11 +102,11 @@
     for pair in range(2):
         parts = [held[(pair * U + u) * 8 : (pair * U + u + 1) * 8, :] for u in range(U)]
         spun = [None] * K0
-        for k0 in range(K0 // 2):
+        for k0 in range(K0 // 4):
             sums = []
-            for start in (0, 1):
+            for start in range(4):
                 real = imag = None
-                for u in range(start, U, 2):
+                for u in range(start, U, 4):
                     cosine, sine = turn(u, k0)
                     term_real = parts[u] if u == 0 else parts[u] * cosine
                     real = term_real if real is None else real + term_real
@@ -114,9 +114,15 @@
                         term_imag = parts[u] * sine
                         imag = term_imag if imag is None else imag + term_imag
                 sums.append((real, imag))
-            (even_real, even_imag), (odd_real, odd_imag) = sums
-            spun[k0] = (even_real + odd_real, even_imag + odd_imag)
-            spun[k0 + K0 // 2] = (even_real - odd_real, even_imag - odd_imag)
+            zero, one, two, three = sums
+            even = (zero[0] + two[0], zero[1] + two[1])
+            odd = (one[0] + three[0], one[1] + three[1])
+            even_gap = (zero[0] - two[0], zero[1] - two[1])
+            odd_gap = (three[1] - one[1], one[0] - three[0])
+            spun[k0] = (even[0] + odd[0], even[1] + odd[1])
+            spun[k0 + 2] = (even_gap[0] + odd_gap[0], even_gap[1] + odd_gap[1])
+            spun[k0 + 4] = (even[0] - odd[0], even[1] - odd[1])
+            spun[k0 + 6] = (even_gap[0] - odd_gap[0], even_gap[1] - odd_gap[1])
         reals, imags = [], []
         for k0 in range(K0):
             cosine = twiddle[k0 : k0 + 1, :]

time: 52.1 us -> 52.1 us (level)
  no operation moved by 1% of the time
where the time goes in v9:
time: 52.1 us; the launch traced here: 51.9 us
  blocking collectives  48.8 us (94%)
  Pallas kernels  3.05 us (6%)
    all_to_all x1, blocking collectives, per_device(): lax.all_to_all(spectra.reshape(ROOTS, 2, LANES), ('limb', 'coef'), 0, 0)  31 us
    all_to_all x1, blocking collectives, per_device(): lax.all_to_all(scaled.reshape(ROOTS, 1, LANES), ('limb', 'coef'), 0, 0)  17.8 us
    pallas_call x1, Pallas kernels, per_device(): pl.pallas_call(evaluate_kernel, out_shape=jax.ShapeDtypeStruct((2 * ROOTS...  1.25 us

profile of v9, /device:TPU:1, one launch (start us, length us, event | category | flops | bytes accessed | tf_op | source)
XLA Modules:
  0.0 51.9 jit_solution(409864351344792568)
XLA Ops:
  0.0 1.3 %evaluate.1 = f32[512,128]{1,0:T(8,128)S(1)} custom-call(f32[2,2,2,1024]{3,2,1,0:T(2,128)} %first_far.1, f32[2,2,2,1024]{3,2,1,0:T(2,128)} %second_far.1, f32[2,16]{1,0:T(2,128)} %bitcast.13, f32[2,16]{1,0:T(2,128)} %bitcast.14, bf16[128,256]{1,0:T(8,128)(2,1)} %constant.6.clone.high_far.wide_high, bf16[128,256]{1,0:T(8,128)(2,1)} %constant.7.clone.low_far.wide_low, ...), custom_call_target="tpu_custom_call" | custom-call | tf_op jit(solution)/shard_map/evaluate/pallas_call | solution.py:353
  1.3 0.0 copy-start.3
  1.3 31.0 %all_to_all.10 = f32[256,2,128]{2,1,0:T(2,128)S(1)} all-to-all(f32[256,2,128]{2,1,0:T(2,128)S(1)} %bitcast.9), channel_id=1, replica_groups=mesh['limb'=8,'coef'=32] {'limb','coef'}, dimensions={0} | all-to-all | bytes 524288 | tf_op jit(solution)/shard_map/all_to_all | solution.py:372
  32.2 0.0 copy-done.3
  32.2 0.9 %tensor.1 = f32[256,128]{1,0:T(8,128)S(1)} custom-call(f32[512,128]{1,0:T(8,128)S(1)} %bitcast.10, f32[16,16]{1,0:T(8,128)S(1)} %copy-done.3), custom_call_target="tpu_custom_call" | custom-call | tf_op jit(solution)/shard_map/tensor/pallas_call | solution.py:373
  33.1 0.0 copy-start
  33.1 0.0 copy-start.1
  33.2 0.0 copy-start.2
  33.2 17.8 %all_to_all.11 = f32[256,1,128]{2,1,0:T(1,128)S(1)} all-to-all(f32[256,1,128]{2,1,0:T(1,128)S(1)} %bitcast.11), channel_id=1, replica_groups=mesh['limb'=8,'coef'=32] {'limb','coef'}, dimensions={0} | all-to-all | bytes 262144 | tf_op jit(solution)/shard_map/all_to_all | solution.py:381
  51.0 0.0 copy-done
  51.0 0.0 copy-done.1
  51.0 0.0 copy-done.2
  51.0 0.9 %restore.1 = f32[2,3,2,1024]{3,2,1,0:T(2,128)} custom-call(f32[256,128]{1,0:T(8,128)S(1)} %bitcast.12, bf16[128,256]{1,0:T(8,128)(2,1)S(1)} %copy-done.1, bf16[128,256]{1,0:T(8,128)(2,1)S(1)} %copy-done, f32[16,128]{1,0:T(8,128)S(1)} %copy-done.2), custom_call_target="tpu_custom_call" | custom-call | tf_op jit(solution)/shard_map/restore/pallas_call | solution.py:382
Async XLA Ops:
  1.3 31.0 %copy-start.3 = (f32[16,16]{1,0:T(8,128)S(1)}, f32[16,16]{1,0:T(8,128)}, u32[]{:S(2)}) copy-start(f32[16,16]{1,0:T(8,128)} %to_special.1) | copy-start | bytes 3076
  33.1 17.9 %copy-start = (bf16[128,256]{1,0:T(8,128)(2,1)S(1)}, bf16[128,256]{1,0:T(8,128)(2,1)}, u32[]{:S(2)}) copy-start(bf16[128,256]{1,0:T(8,128)(2,1)} %constant.7.clone.low_far.wide_low) | copy-start | bytes 196612
  33.1 17.9 %copy-start.1 = (bf16[128,256]{1,0:T(8,128)(2,1)S(1)}, bf16[128,256]{1,0:T(8,128)(2,1)}, u32[]{:S(2)}) copy-start(bf16[128,256]{1,0:T(8,128)(2,1)} %constant.6.clone.high_far.wide_high) | copy-start | bytes 196612
  33.2 17.8 %copy-start.2 = (f32[16,128]{1,0:T(8,128)S(1)}, f32[16,128]{1,0:T(8,128)}, u32[]{:S(2)}) copy-start(f32[16,128]{1,0:T(8,128)} %constant.8.clone.twiddle_far.twiddle) | copy-start | bytes 24580

commit v10 on v9

--- a/solution.py
+++ b/solution.py
@@ -369,7 +369,7 @@
         compiler_params=params,
         name="evaluate",
     )(*kept_far(first_cipher, second_cipher, keep_table.T, scale_table.T, wide_high, wide_low, twiddle))
-    spread = lax.all_to_all(spectra.reshape(ROOTS, 2, LANES), ("limb", "coef"), 0, 0)
+    spread = lax.all_to_all(spectra.reshape(ROOTS, 1, 2 * LANES), ("limb", "coef"), 0, 0)
     scaled = pl.pallas_call(
         tensor_kernel,
         out_shape=jax.ShapeDtypeStruct((ROOTS, LANES), f32),

time: 52.1 us -> 52.1 us (level)
  no operation moved by 1% of the time
where the time goes in v10:
time: 52.1 us; the launch traced here: 51.9 us
  blocking collectives  48.8 us (94%)
  Pallas kernels  3.05 us (6%)
    all_to_all x1, blocking collectives, per_device(): lax.all_to_all(spectra.reshape(ROOTS, 1, 2 * LANES), ('limb', 'coef'), 0, 0)  31 us
    all_to_all x1, blocking collectives, per_device(): lax.all_to_all(scaled.reshape(ROOTS, 1, LANES), ('limb', 'coef'), 0, 0)  17.8 us
    pallas_call x1, Pallas kernels, per_device(): pl.pallas_call(evaluate_kernel, out_shape=jax.ShapeDtypeStruct((2 * ROOTS...  1.25 us

profile of v10, /device:TPU:1, one launch (start us, length us, event | category | flops | bytes accessed | tf_op | source)
XLA Modules:
  0.0 51.9 jit_solution(409864351344792568)
XLA Ops:
  0.0 1.3 %evaluate.1 = f32[512,128]{1,0:T(8,128)S(1)} custom-call(f32[2,2,2,1024]{3,2,1,0:T(2,128)} %first_far.1, f32[2,2,2,1024]{3,2,1,0:T(2,128)} %second_far.1, f32[2,16]{1,0:T(2,128)} %bitcast.13, f32[2,16]{1,0:T(2,128)} %bitcast.14, bf16[128,256]{1,0:T(8,128)(2,1)} %constant.6.clone.high_far.wide_high, bf16[128,256]{1,0:T(8,128)(2,1)} %constant.7.clone.low_far.wide_low, ...), custom_call_target="tpu_custom_call" | custom-call | tf_op jit(solution)/shard_map/evaluate/pallas_call | solution.py:353
  1.3 0.0 copy-start.3
  1.3 31.0 %all_to_all.10 = f32[256,1,256]{2,1,0:T(1,128)S(1)} all-to-all(f32[256,1,256]{2,1,0:T(1,128)S(1)} %bitcast.9), channel_id=1, replica_groups=mesh['limb'=8,'coef'=32] {'limb','coef'}, dimensions={0} | all-to-all | bytes 524288 | tf_op jit(solution)/shard_map/all_to_all | solution.py:372
  32.2 0.0 copy-done.3
  32.2 0.9 %tensor.1 = f32[256,128]{1,0:T(8,128)S(1)} custom-call(f32[512,128]{1,0:T(8,128)S(1)} %bitcast.10, f32[16,16]{1,0:T(8,128)S(1)} %copy-done.3), custom_call_target="tpu_custom_call" | custom-call | tf_op jit(solution)/shard_map/tensor/pallas_call | solution.py:373
  33.1 0.0 copy-start
  33.1 0.0 copy-start.1
  33.2 0.0 copy-start.2
  33.2 17.8 %all_to_all.11 = f32[256,1,128]{2,1,0:T(1,128)S(1)} all-to-all(f32[256,1,128]{2,1,0:T(1,128)S(1)} %bitcast.11), channel_id=1, replica_groups=mesh['limb'=8,'coef'=32] {'limb','coef'}, dimensions={0} | all-to-all | bytes 262144 | tf_op jit(solution)/shard_map/all_to_all | solution.py:381
  51.0 0.0 copy-done
  51.0 0.0 copy-done.1
  51.0 0.0 copy-done.2
  51.0 0.9 %restore.1 = f32[2,3,2,1024]{3,2,1,0:T(2,128)} custom-call(f32[256,128]{1,0:T(8,128)S(1)} %bitcast.12, bf16[128,256]{1,0:T(8,128)(2,1)S(1)} %copy-done.1, bf16[128,256]{1,0:T(8,128)(2,1)S(1)} %copy-done, f32[16,128]{1,0:T(8,128)S(1)} %copy-done.2), custom_call_target="tpu_custom_call" | custom-call | tf_op jit(solution)/shard_map/restore/pallas_call | solution.py:382
Async XLA Ops:
  1.3 31.0 %copy-start.3 = (f32[16,16]{1,0:T(8,128)S(1)}, f32[16,16]{1,0:T(8,128)}, u32[]{:S(2)}) copy-start(f32[16,16]{1,0:T(8,128)} %to_special.1) | copy-start | bytes 3076
  33.1 17.9 %copy-start = (bf16[128,256]{1,0:T(8,128)(2,1)S(1)}, bf16[128,256]{1,0:T(8,128)(2,1)}, u32[]{:S(2)}) copy-start(bf16[128,256]{1,0:T(8,128)(2,1)} %constant.7.clone.low_far.wide_low) | copy-start | bytes 196612
  33.1 17.9 %copy-start.1 = (bf16[128,256]{1,0:T(8,128)(2,1)S(1)}, bf16[128,256]{1,0:T(8,128)(2,1)}, u32[]{:S(2)}) copy-start(bf16[128,256]{1,0:T(8,128)(2,1)} %constant.6.clone.high_far.wide_high) | copy-start | bytes 196612
  33.2 17.8 %copy-start.2 = (f32[16,128]{1,0:T(8,128)S(1)}, f32[16,128]{1,0:T(8,128)}, u32[]{:S(2)}) copy-start(f32[16,128]{1,0:T(8,128)} %constant.8.clone.twiddle_far.twiddle) | copy-start | bytes 24580

commit v11 on v9

--- a/solution.py
+++ b/solution.py
@@ -309,22 +309,11 @@
         for k0 in range(K0 // 2):
             one, two = turned[k0], turned[k0 + K0 // 2]
             halves.append(((one[0] + two[0], one[1] + two[1]), (one[0] - two[0], one[1] - two[1])))
-        quarters = []
-        for k0 in range(K0 // 4):
-            (even, odd), (even_far, odd_far) = halves[k0], halves[k0 + 2]
-            quarters.append(
-                (
-                    (even[0] + even_far[0], even[1] + even_far[1]),
-                    (odd[0] + odd_far[1], odd[1] - odd_far[0]),
-                    (even[0] - even_far[0], even[1] - even_far[1]),
-                    (odd[0] - odd_far[1], odd[1] + odd_far[0]),
-                )
-            )
         for u in range(U):
             total = None
-            for k0 in range(K0 // 4):
+            for k0 in range(K0 // 2):
                 cosine, sine = turn(u, k0)
-                real_part, imag_part = quarters[k0][u % 4]
+                real_part, imag_part = halves[k0][u % 2]
                 term = real_part if u == 0 else real_part * cosine + imag_part * sine
                 total = term if total is None else total + term
             total = jnp.where(middle, total + pltpu.roll(total, 6, 0), total)

time: 52.1 us -> 52.2 us (level)
  no operation moved by 1% of the time
where the time goes in v11:
time: 52.2 us; the launch traced here: 51.9 us
  blocking collectives  48.8 us (93%)
  Pallas kernels  3.06 us (6%)
    all_to_all x1, blocking collectives, per_device(): lax.all_to_all(spectra.reshape(ROOTS, 2, LANES), ('limb', 'coef'), 0, 0)  31 us
    all_to_all x1, blocking collectives, per_device(): lax.all_to_all(scaled.reshape(ROOTS, 1, LANES), ('limb', 'coef'), 0, 0)  17.8 us
    pallas_call x1, Pallas kernels, per_device(): pl.pallas_call(evaluate_kernel, out_shape=jax.ShapeDtypeStruct((2 * ROOTS...  1.25 us

profile of v11, /device:TPU:1, one launch (start us, length us, event | category | flops | bytes accessed | tf_op | source)
XLA Modules:
  0.0 51.9 jit_solution(14514756080550041120)
XLA Ops:
  0.0 1.3 %evaluate.1 = f32[512,128]{1,0:T(8,128)S(1)} custom-call(f32[2,2,2,1024]{3,2,1,0:T(2,128)} %first_far.1, f32[2,2,2,1024]{3,2,1,0:T(2,128)} %second_far.1, f32[2,16]{1,0:T(2,128)} %bitcast.13, f32[2,16]{1,0:T(2,128)} %bitcast.14, bf16[128,256]{1,0:T(8,128)(2,1)} %constant.6.clone.high_far.wide_high, bf16[128,256]{1,0:T(8,128)(2,1)} %constant.7.clone.low_far.wide_low, ...), custom_call_target="tpu_custom_call" | custom-call | tf_op jit(solution)/shard_map/evaluate/pallas_call | solution.py:342
  1.3 0.0 copy-start.3
  1.3 31.0 %all_to_all.10 = f32[256,2,128]{2,1,0:T(2,128)S(1)} all-to-all(f32[256,2,128]{2,1,0:T(2,128)S(1)} %bitcast.9), channel_id=1, replica_groups=mesh['limb'=8,'coef'=32] {'limb','coef'}, dimensions={0} | all-to-all | bytes 524288 | tf_op jit(solution)/shard_map/all_to_all | solution.py:361
  32.2 0.0 copy-done.3
  32.2 0.9 %tensor.1 = f32[256,128]{1,0:T(8,128)S(1)} custom-call(f32[512,128]{1,0:T(8,128)S(1)} %bitcast.10, f32[16,16]{1,0:T(8,128)S(1)} %copy-done.3), custom_call_target="tpu_custom_call" | custom-call | tf_op jit(solution)/shard_map/tensor/pallas_call | solution.py:362
  33.1 0.0 copy-start
  33.1 0.0 copy-start.1
  33.2 0.0 copy-start.2
  33.2 17.8 %all_to_all.11 = f32[256,1,128]{2,1,0:T(1,128)S(1)} all-to-all(f32[256,1,128]{2,1,0:T(1,128)S(1)} %bitcast.11), channel_id=1, replica_groups=mesh['limb'=8,'coef'=32] {'limb','coef'}, dimensions={0} | all-to-all | bytes 262144 | tf_op jit(solution)/shard_map/all_to_all | solution.py:370
  51.0 0.0 copy-done
  51.0 0.0 copy-done.1
  51.0 0.0 copy-done.2
  51.0 0.9 %restore.1 = f32[2,3,2,1024]{3,2,1,0:T(2,128)} custom-call(f32[256,128]{1,0:T(8,128)S(1)} %bitcast.12, bf16[128,256]{1,0:T(8,128)(2,1)S(1)} %copy-done.1, bf16[128,256]{1,0:T(8,128)(2,1)S(1)} %copy-done, f32[16,128]{1,0:T(8,128)S(1)} %copy-done.2), custom_call_target="tpu_custom_call" | custom-call | tf_op jit(solution)/shard_map/restore/pallas_call | solution.py:371
Async XLA Ops:
  1.3 31.0 %copy-start.3 = (f32[16,16]{1,0:T(8,128)S(1)}, f32[16,16]{1,0:T(8,128)}, u32[]{:S(2)}) copy-start(f32[16,16]{1,0:T(8,128)} %to_special.1) | copy-start | bytes 3076
  33.1 17.9 %copy-start = (bf16[128,256]{1,0:T(8,128)(2,1)S(1)}, bf16[128,256]{1,0:T(8,128)(2,1)}, u32[]{:S(2)}) copy-start(bf16[128,256]{1,0:T(8,128)(2,1)} %constant.7.clone.low_far.wide_low) | copy-start | bytes 196612
  33.1 17.9 %copy-start.1 = (bf16[128,256]{1,0:T(8,128)(2,1)S(1)}, bf16[128,256]{1,0:T(8,128)(2,1)}, u32[]{:S(2)}) copy-start(bf16[128,256]{1,0:T(8,128)(2,1)} %constant.6.clone.high_far.wide_high) | copy-start | bytes 196612
  33.2 17.8 %copy-start.2 = (f32[16,128]{1,0:T(8,128)S(1)}, f32[16,128]{1,0:T(8,128)}, u32[]{:S(2)}) copy-start(f32[16,128]{1,0:T(8,128)} %constant.8.clone.twiddle_far.twiddle) | copy-start | bytes 24580
